TPU v7x, 256 devices: a whole 4x4x8 slice. The times are simulated.
256 devices in a mesh: gx: 4 (over x), gy: 8 (over y, core), gz: 8 (over z).
Axes of the slice: x: 4, y: 4, z: 8, core: 2. Of those that a mesh axis runs over, the one named last changes fastest.
Arguments:
- panel: float32 [4, 8, 32, 256, 256], P('gx', 'gy', 'gz'), may hold values from -120 to 120
- tiles: float32 [4, 8, 32, 10, 256, 256], P('gx', 'gy', 'gz'), may hold values from -0.125 to 0.125
- codes: int32 [4, 8, 32, 10], P('gx', 'gy', 'gz'), may hold values from 0 to 26, as said below
Outputs:
- bands: float32 [4, 8, 32, 256, 256], P('gx', 'gy', 'gz')
- factor: float32 [256, 256], replicated
Inputs may be any that keep to these rules, and one draw needn't show every extreme that they name: Slot 0 of every element holds 13, the element itself; the other 9 slots of an element hold distinct codes other than 13.
All inputs are finite; a program needn't handle non-finite values.
Results may differ from a plain program's by a relative error of at most 0.0003.
Values sent between devices are 32-bit elements; how exact they have to be, the bound alone decides.
No kernel may reach another device: no remote copies, remote signals or barrier semaphores. Data moves between devices by JAX's collectives and lax.ppermute only.
A program may use at most 128 MiB of HBM per device.

v0:
```python
import jax
import jax.numpy as jnp
from jax import lax
from jax.sharding import PartitionSpec as P


def padded_2(shard, sides, width):
    for axis, dim in sides:
        peers, length = (lax.axis_size(axis), shard.shape[dim])
        up = [(i, (i + 1) % peers) for i in range(peers - 1)]
        down = [(j, i) for i, j in up]
        last = lax.slice_in_dim(shard, length - width, length, axis=dim)
        initial = lax.slice_in_dim(shard, 0, width, axis=dim)
        before = lax.ppermute(last, axis, up)
        after = lax.ppermute(initial, axis, down)
        shard = jnp.concatenate([before, shard, after], axis=dim)
    return shard


def window(padded, first, second, third):
    zero = jnp.zeros((), jnp.int32)
    piece = lax.dynamic_slice(
        padded, (first, second, third, zero, zero), (1, 1, 1, padded.shape[3], padded.shape[4])
    )
    return piece[0, 0, 0]


def per_device(panel, tiles, codes):
    along_x = padded_2(panel, (("gx", 0),), 1)
    along_y = padded_2(along_x, (("gy", 1),), 1)
    padded = padded_2(along_y, (("gz", 2),), 1)
    width = panel.shape[4]
    products = []
    for element_cell in range(panel.shape[2]):
        slot_codes = codes[0, 0, element_cell]
        windows = jax.vmap(lambda c: window(padded, c // 9, c // 3 % 3, element_cell + c % 3))(
            slot_codes
        )
        applied = jnp.einsum(
            "kab,kbc->ac", tiles[0, 0, element_cell], windows, precision=lax.Precision.HIGHEST
        )
        products.append(applied - 0.5 * panel[0, 0, element_cell])
    filtered = jnp.stack(products)
    flat_rows = filtered.reshape(-1, width)
    local_gram = jnp.dot(flat_rows.T, flat_rows, precision=lax.Precision.HIGHEST)
    row_total = flat_rows.shape[0] * lax.axis_size("gx") * lax.axis_size("gy") * lax.axis_size("gz")
    summed = lax.psum(local_gram, ("gx", "gy", "gz"))
    gram = summed / row_total
    lower = jnp.linalg.cholesky(gram)
    inverse = lax.linalg.triangular_solve(
        lower, jnp.eye(width, dtype=gram.dtype), left_side=True, lower=True
    )
    bands = jnp.dot(flat_rows, inverse.T, precision=lax.Precision.HIGHEST).reshape(panel.shape)
    return (bands, lower.T)


def solution(mesh):
    in_specs = (
        P("gx", "gy", "gz", None, None),
        P("gx", "gy", "gz", None, None, None),
        P("gx", "gy", "gz", None),
    )
    out_specs = (P("gx", "gy", "gz", None, None), P())
    return jax.shard_map(
        per_device, mesh=mesh, in_specs=in_specs, out_specs=out_specs, check_vma=False
    )
```

profile of v0, /device:TPU:1, one launch (start us, length us, event | category | flops | bytes accessed | tf_op | source)
XLA Modules:
  0.0 531.8 jit_solution(13303097579600552157)
XLA Ops:
  7.2 0.0 all-reduce.3.cloned.1.call-start
  7.2 0.0 copy-start.4
  7.2 4.1 collective-permute-start
  11.4 1.3 collective-permute-start.1
  12.7 20.8 %collective-permute-done = f32[1,1,4,256,256]{4,3,2,1,0:T(8,128)S(1)} collective-permute-done((f32[1,1,4,256,256]{4,3,2,1,0:T(8,128)}, f32[1,1,4,256,256]{4,3,2,1,0:T(8,128)S(1)}, u32[]{:S(2)}, u32[]{:S(2)}) %collective-permute-start) | collective-permute-done | bytes 1048608 | tf_op jit(solution)/shard_map/ppermute | solution.py:14
  33.4 0.1 constant_dynamic-update-slice_fusion.2
  33.5 0.0 copy-done.4
  33.5 0.1 constant_dynamic-update-slice_fusion.1
  33.6 3.6 collective-permute-done.1
  37.2 0.1 constant_dynamic-update-slice_fusion
  37.3 5.0 collective-permute-start.2
  42.2 1.9 collective-permute-start.3
  44.2 32.3 %collective-permute-done.2 = f32[3,1,4,256,256]{4,3,2,1,0:T(8,128)S(1)} collective-permute-done((f32[3,1,4,256,256]{4,3,2,1,0:T(8,128)S(1)}, f32[3,1,4,256,256]{4,3,2,1,0:T(8,128)S(1)}, u32[]{:S(2)}, u32[]{:S(2)}) %collective-permute-start.2) | collective-permute-done | bytes 3145760 | tf_op jit(solution)/shard_map/ppermute | solution.py:14
  76.4 4.8 collective-permute-done.3
  81.2 2.8 pad_maximum_fusion.3
  84.0 0.0 copy-done
  84.0 0.2 copy-done.1
  84.2 5.1 collective-permute-start.4
  89.3 1.3 collective-permute-start.5
  90.6 0.9 fusion.104
  91.5 0.9 copy.29
  92.4 1.1 copy.28
  93.5 1.8 copy.27
  95.3 1.8 copy.26
  97.1 0.0 copy-done.8
  97.1 0.1 fusion.100
  97.1 16.9 %collective-permute-done.4 = f32[3,3,1,256,256]{4,3,2,1,0:T(8,128)} collective-permute-done((f32[3,3,1,256,256]{4,3,2,1,0:T(8,128)}, f32[3,3,1,256,256]{4,3,2,1,0:T(8,128)}, u32[]{:S(2)}, u32[]{:S(2)}) %collective-permute-start.4) | collective-permute-done | bytes 2359328 | tf_op jit(solution)/shard_map/ppermute | solution.py:14
  114.0 5.2 collective-permute-done.5
  119.2 9.8 %pad_maximum_fusion = f32[3,3,6,256,256]{4,3,2,1,0:T(8,128)} fusion(f32[3,3,1,256,256]{4,3,2,1,0:T(8,128)} %collective-permute-done.5, f32[3,1,4,256,256]{4,3,2,1,0:T(8,128)} %copy-done.1, f32[3,1,4,256,256]{4,3,2,1,0:T(8,128)S(1)} %constant_dynamic-update-slice_fusion, f32[3,1,4,256,256]{4,3,2,1,0:T(8,128)} %copy-done, ...), kind=kLoop, calls=%fused_computation.6 | loop fusion | flops 14155776 | bytes 28311552 | tf_op jit(solution)/shard_map/concatenate | solution.py:16
  129.1 7.3 %gather_fusion.3 = f32[10,256,256]{2,1,0:T(8,128)} fusion(f32[3,3,6,256,256]{4,3,2,1,0:T(8,128)} %pad_maximum_fusion, s32[10]{0:T(128)S(1)} %get-tuple-element.36), kind=kCustom, calls=%fused_computation.3 | custom fusion | bytes 5243080 | tf_op jit(solution)/shard_map/vmap()/gather | solution.py:22
  136.4 7.4 %gather_fusion.2 = f32[10,256,256]{2,1,0:T(8,128)} fusion(f32[3,3,6,256,256]{4,3,2,1,0:T(8,128)} %pad_maximum_fusion, s32[10]{0:T(128)S(1)} %get-tuple-element.37), kind=kCustom, calls=%fused_computation.2 | custom fusion | bytes 5243080 | tf_op jit(solution)/shard_map/vmap()/gather | solution.py:22
  143.7 5.7 %gather_fusion.1 = f32[10,256,256]{2,1,0:T(8,128)S(1)} fusion(f32[3,3,6,256,256]{4,3,2,1,0:T(8,128)} %pad_maximum_fusion, s32[10]{0:T(128)S(1)} %get-tuple-element.35), kind=kCustom, calls=%fused_computation.1 | custom fusion | bytes 5243080 | tf_op jit(solution)/shard_map/vmap()/gather | solution.py:22
  149.5 0.0 copy-start.7
  149.5 7.4 %gather_fusion = f32[10,256,256]{2,1,0:T(8,128)} fusion(f32[3,3,6,256,256]{4,3,2,1,0:T(8,128)} %pad_maximum_fusion, s32[10]{0:T(128)S(1)} %get-tuple-element.34), kind=kCustom, calls=%fused_computation | custom fusion | bytes 5243080 | tf_op jit(solution)/shard_map/vmap()/gather | solution.py:22
  156.9 0.0 copy-done.7
  156.9 7.0 %fusion.27 = f32[1,256,256]{1,2,0:T(8,128)S(1)} fusion(f32[10,256,256]{2,1,0:T(8,128)} %gather_fusion.3, f32[1,1,4,10,256,256]{5,4,3,2,1,0:T(8,128)} %param.4, f32[1,1,1,256,256]{3,4,2,1,0:T(8,128)S(1)} %copy-done.7), kind=kOutput, calls=%fused_computation.29 | convolution fusion | flops 2013396992 | bytes 5767168 | tf_op jit(solution)/shard_map/kab,kbc->ac/dot_general | solution.py:39
  163.9 0.0 copy-start.5
  163.9 6.2 %fusion.33 = f32[1,256,256]{1,2,0:T(8,128)S(1)} fusion(f32[10,256,256]{2,1,0:T(8,128)S(1)} %copy-done.3, f32[1,1,4,10,256,256]{5,4,3,2,1,0:T(8,128)} %param.4, f32[1,1,1,256,256]{3,4,2,1,0:T(8,128)S(1)} %copy.28), kind=kOutput, calls=%fused_computation.31 | convolution fusion | flops 2013396992 | bytes 5767168 | tf_op jit(solution)/shard_map/kab,kbc->ac/dot_general | solution.py:39
  170.2 6.3 %fusion.39 = f32[1,256,256]{1,2,0:T(8,128)S(1)} fusion(f32[10,256,256]{2,1,0:T(8,128)S(1)} %gather_fusion.1, f32[1,1,4,10,256,256]{5,4,3,2,1,0:T(8,128)} %param.4, f32[1,1,1,256,256]{3,4,2,1,0:T(8,128)S(1)} %copy-done.5), kind=kOutput, calls=%fused_computation.33 | convolution fusion | flops 2013396992 | bytes 5767168 | tf_op jit(solution)/shard_map/kab,kbc->ac/dot_general | solution.py:39
  176.5 6.2 %fusion.45 = f32[1,256,256]{1,2,0:T(8,128)S(1)} fusion(f32[10,256,256]{2,1,0:T(8,128)S(1)} %copy-done.2, f32[1,1,4,10,256,256]{5,4,3,2,1,0:T(8,128)} %param.4, f32[1,1,1,256,256]{3,4,2,1,0:T(8,128)S(1)} %copy-done.6), kind=kOutput, calls=%fused_computation.35 | convolution fusion | flops 2013396992 | bytes 5767168 | tf_op jit(solution)/shard_map/kab,kbc->ac/dot_general | solution.py:39
  182.7 1.7 convolution_bitcast_fusion.1
  184.5 0.0 all-reduce.3.cloned.1.call-update
  184.6 274.1 %all-reduce.3.cloned.1.call-done = f32[256,256]{0,1:T(8,128)} async-done(((f32[256,256]{0,1:T(8,128)}), f32[256,256]{0,1:T(8,128)}) %all-reduce.3.cloned.1.call-update) | async-done | bytes 262160 | tf_op jit(solution)/shard_map/psum | solution.py:47
  458.7 1.0 broadcast_multiply_fusion
  459.6 0.1 copy.15
  459.8 1.0 fusion.50
  460.8 11.7 %cholesky.50 = f32[128,128]{1,0:T(8,128)S(1)} custom-call(f32[128,128]{1,0:T(8,128)S(1)} %cholesky.118), custom_call_target="Cholesky" | custom-call | tf_op jit(solution)/shard_map/jit(cholesky)/cholesky | solution.py:49
  472.5 10.0 %custom-call.14 = f32[1,128,128]{1,2,0:T(8,128)S(1)} custom-call(f32[1,128,128]{2,1,0:T(8,128)S(1)} %get-tuple-element.33), custom_call_target="InvertDiagBlocksLowerTriangular" | custom-call | tf_op jit(solution)/shard_map/jit(cholesky)/cholesky | solution.py:49
  482.5 0.2 constant_dynamic-update-slice_fusion.4
  482.7 0.3 convolution_subtract_fusion.1
  483.0 11.7 %cholesky.105 = f32[128,128]{1,0:T(8,128)S(1)} custom-call(f32[128,128]{1,0:T(8,128)S(1)} %convolution_subtract_fusion.1), custom_call_target="Cholesky" | custom-call | tf_op jit(solution)/shard_map/jit(cholesky)/cholesky | solution.py:49
  494.8 0.6 compare_reduce_fusion
  496.7 0.1 triangular_solve.63
  496.7 3.8 while.1
  496.8 0.6 fusion.114
  497.3 1.3 bitcast_dynamic-update-slice_fusion.2
  498.7 0.6 fusion.114
  499.3 1.3 bitcast_dynamic-update-slice_fusion.2
  500.6 19.7 %custom-call.15 = f32[2,128,128]{1,2,0:T(8,128)S(1)} custom-call(f32[2,128,128]{2,1,0:T(8,128)S(1)} %get-tuple-element.9), custom_call_target="InvertDiagBlocksLowerTriangular" | custom-call | tf_op jit(solution)/shard_map/triangular_solve | solution.py:50
  520.3 0.3 fusion.53
  520.5 0.3 convolution_subtract_fusion
  520.8 0.3 fusion.56
  521.1 2.8 convolution_bitcast_fusion
  523.9 0.8 copy.17
  (20 shorter events, 0.2 us)
Async XLA Ops:
  7.2 451.5 %all-reduce.3.cloned.1.call-start = ((), (), s32[]{:S(2)}) async-start(), calls=%async_computation | async-start | bytes 524288 | tf_op jit(solution)/shard_map/psum | solution.py:47
  7.2 26.3 %copy-start.4 = (f32[1,1,4,256,256]{4,3,2,1,0:T(8,128)S(1)}, f32[1,1,4,256,256]{4,3,2,1,0:T(8,128)}, u32[]{:S(2)}) copy-start(f32[1,1,4,256,256]{4,3,2,1,0:T(8,128)} %param.3) | copy-start | bytes 3145732
  7.2 26.2 %collective-permute-start = (f32[1,1,4,256,256]{4,3,2,1,0:T(8,128)}, f32[1,1,4,256,256]{4,3,2,1,0:T(8,128)S(1)}, u32[]{:S(2)}, u32[]{:S(2)}) collective-permute-start(f32[1,1,4,256,256]{4,3,2,1,0:T(8,128)} %param.3), channel_id=1, source_target_pairs={{0,64},{64,128},{128,192},{1,65},{65,129},{129,193},{2,66},{66,130... | collective-permute-start | bytes 3145736 | tf_op jit(solution)/shard_map/ppermute | solution.py:14
  11.4 25.8 %collective-permute-start.1 = (f32[1,1,4,256,256]{4,3,2,1,0:T(8,128)}, f32[1,1,4,256,256]{4,3,2,1,0:T(8,128)S(1)}, u32[]{:S(2)}, u32[]{:S(2)}) collective-permute-start(f32[1,1,4,256,256]{4,3,2,1,0:T(8,128)} %param.3), channel_id=1, source_target_pairs={{64,0},{128,64},{192,128},{65,1},{129,65},{193,129},{66,2},{130,66... | collective-permute-start | bytes 3145736 | tf_op jit(solution)/shard_map/ppermute | solution.py:15
  37.3 39.2 %collective-permute-start.2 = (f32[3,1,4,256,256]{4,3,2,1,0:T(8,128)S(1)}, f32[3,1,4,256,256]{4,3,2,1,0:T(8,128)S(1)}, u32[]{:S(2)}, u32[]{:S(2)}) collective-permute-start(f32[3,1,4,256,256]{4,3,2,1,0:T(8,128)S(1)} %constant_dynamic-update-slice_fusion), channel_id=1, source_target_pairs={{0,8},{8,16},{16,24},{24,32},{32,40},{40,48},{48,56},{1,9},{9,17},... | collective-permute-start | bytes 9437192 | tf_op jit(solution)/shard_map/ppermute | solution.py:14
  42.2 39.0 %collective-permute-start.3 = (f32[3,1,4,256,256]{4,3,2,1,0:T(8,128)S(1)}, f32[3,1,4,256,256]{4,3,2,1,0:T(8,128)S(1)}, u32[]{:S(2)}, u32[]{:S(2)}) collective-permute-start(f32[3,1,4,256,256]{4,3,2,1,0:T(8,128)S(1)} %constant_dynamic-update-slice_fusion), channel_id=1, source_target_pairs={{8,0},{16,8},{24,16},{32,24},{40,32},{48,40},{56,48},{9,1},{17,9},... | collective-permute-start | bytes 9437192 | tf_op jit(solution)/shard_map/ppermute | solution.py:15
  76.4 7.6 %copy-start = (f32[3,1,4,256,256]{4,3,2,1,0:T(8,128)}, f32[3,1,4,256,256]{4,3,2,1,0:T(8,128)S(1)}, u32[]{:S(2)}) copy-start(f32[3,1,4,256,256]{4,3,2,1,0:T(8,128)S(1)} %collective-permute-done.2) | copy-start | bytes 9437188
  81.2 3.0 copy-start.1
  84.2 12.8 %copy-start.8 = (s32[1,1,4,10]{3,2,1,0:T(4,128)S(1)}, s32[1,1,4,10]{3,2,1,0:T(4,128)}, u32[]{:S(2)}) copy-start(s32[1,1,4,10]{3,2,1,0:T(4,128)} %param.5) | copy-start | bytes 484
  84.2 29.8 %collective-permute-start.4 = (f32[3,3,1,256,256]{4,3,2,1,0:T(8,128)}, f32[3,3,1,256,256]{4,3,2,1,0:T(8,128)}, u32[]{:S(2)}, u32[]{:S(2)}) collective-permute-start(f32[3,3,1,256,256]{4,3,2,1,0:T(8,128)} %get-tuple-element.22), channel_id=1, source_target_pairs={{0,1},{1,2},{2,3},{3,4},{4,5},{5,6},{6,7},{8,9},{9,10},{10,11},{11... | collective-permute-start | bytes 7077896 | tf_op jit(solution)/shard_map/ppermute | solution.py:14
  89.3 29.9 %collective-permute-start.5 = (f32[3,3,1,256,256]{4,3,2,1,0:T(8,128)}, f32[3,3,1,256,256]{4,3,2,1,0:T(8,128)}, u32[]{:S(2)}, u32[]{:S(2)}) collective-permute-start(f32[3,3,1,256,256]{4,3,2,1,0:T(8,128)} %get-tuple-element.23), channel_id=1, source_target_pairs={{1,0},{2,1},{3,2},{4,3},{5,4},{6,5},{7,6},{9,8},{10,9},{11,10},{12... | collective-permute-start | bytes 7077896 | tf_op jit(solution)/shard_map/ppermute | solution.py:15
  149.5 7.4 %copy-start.7 = (f32[1,1,1,256,256]{3,4,2,1,0:T(8,128)S(1)}, f32[1,1,1,256,256]{3,4,2,1,0:T(8,128)}, u32[]{:S(2)}) copy-start(f32[1,1,1,256,256]{3,4,2,1,0:T(8,128)} %copy.29) | copy-start | bytes 786436
  156.9 7.0 %copy-start.3 = (f32[10,256,256]{2,1,0:T(8,128)S(1)}, f32[10,256,256]{2,1,0:T(8,128)}, u32[]{:S(2)}) copy-start(f32[10,256,256]{2,1,0:T(8,128)} %gather_fusion.2) | copy-start | bytes 7864324
  163.9 6.3 %copy-start.5 = (f32[1,1,1,256,256]{3,4,2,1,0:T(8,128)S(1)}, f32[1,1,1,256,256]{3,4,2,1,0:T(8,128)}, u32[]{:S(2)}) copy-start(f32[1,1,1,256,256]{3,4,2,1,0:T(8,128)} %copy.27) | copy-start | bytes 786436
  170.2 6.4 %copy-start.2 = (f32[10,256,256]{2,1,0:T(8,128)S(1)}, f32[10,256,256]{2,1,0:T(8,128)}, u32[]{:S(2)}) copy-start(f32[10,256,256]{2,1,0:T(8,128)} %gather_fusion) | copy-start | bytes 7864324
  170.2 6.4 %copy-start.6 = (f32[1,1,1,256,256]{3,4,2,1,0:T(8,128)S(1)}, f32[1,1,1,256,256]{3,4,2,1,0:T(8,128)}, u32[]{:S(2)}) copy-start(f32[1,1,1,256,256]{3,4,2,1,0:T(8,128)} %copy.26) | copy-start | bytes 786436
Sparse Core Ops, SparseCore 0:
  184.6 273.9 all-reduce.2
where the time goes:
time: 536 us; the launch traced here: 532 us
  waiting for transfers between devices  358 us (67%)
  other arithmetic  68.5 us (13%)
  local copies, waits for them, and re-layouts  39.6 us (7%)
  matrix products  31.6 us (6%)
  starting transfers between devices  18.7 us (3%)
  between operations  15.8 us (3%)
    psum x1, waiting for transfers between devices, per_device(): summed = lax.psum(local_gram, ('gx', 'gy', 'gz'))  274 us
    ppermute x3, waiting for transfers between devices, padded_2(): before = lax.ppermute(last, axis, up)  69.9 us
    another operation x6, other arithmetic, per_device(): lower = jnp.linalg.cholesky(gram)  34.1 us
    gather x4, local copies, waits for them, and re-layouts, window(): lax.dynamic_slice(padded, (first, second, third, zero, zero), (1, 1, 1, p...  27.8 us
    dot_general x4, matrix products, per_device(): jnp.einsum('kab,kbc->ac', tiles[0, 0, element_cell], windows, precision=l...  25.7 us
    another operation x2, other arithmetic, per_device(): lax.linalg.triangular_solve(lower, jnp.eye(width, dtype=gram.dtype), left...  19.7 us
    ppermute x3, starting transfers between devices, padded_2(): before = lax.ppermute(last, axis, up)  14.2 us
    ppermute x3, waiting for transfers between devices, padded_2(): after = lax.ppermute(initial, axis, down)  13.6 us
  transfers between devices with their start and end apart: 7, of which 7 were waited for; matrix products, arithmetic and copies ran while one was open for 1% of the time, Pallas kernels for 0%

commit v1 on v0

v1 whole, which is shorter than its diff:
```python
import functools

import jax
import jax.numpy as jnp
import numpy as np
from jax import lax
from jax.experimental import pallas as pl
from jax.experimental.pallas import tpu as pltpu
from jax.sharding import PartitionSpec as P

F32 = jnp.float32
BF16 = jnp.bfloat16
EXACT = lax.Precision.HIGHEST
CELLS = 4
SLOTS = 10
SIDE = 256
BLOCK = 64

EARLY = (
    ("own", 4), ("o", 4), ("i", 4), ("below", 1), ("above", 1), ("ends-", 2), ("ends+", 2),
    ("mids-", 2), ("mids+", 2), ("o_ends", 4), ("below2", 3), ("above2", 3), ("i2", 6),
)
LATE = (("o_mids", 4), ("below3", 2), ("above3", 2), ("i3", 8))


def place(column, dx, z):
    side = int(dx > 0)
    sign = "+" if dx > 0 else "-"
    last = int(z == CELLS - 1)
    inside = 0 <= z < CELLS
    mid = z in (1, 2)
    outer = "below" if z < 0 else "above"
    if column == "own":
        if dx == 0:
            return ("own", z) if inside else (outer, 0)
        if inside:
            return ("mids" + sign, z - 1) if mid else ("ends" + sign, last)
        return (outer + "2", side)
    if column == "o":
        if dx == 0:
            return ("o", z) if inside else (outer + "2", 2)
        if inside:
            return ("o_mids", 2 * side + z - 1) if mid else ("o_ends", 2 * side + last)
        return (outer + "3", side)
    if dx == 0:
        return ("i", z) if inside else ("i2", 4 + int(z > 0))
    if inside:
        return ("i3", 2 * side + z - 1) if mid else ("i2", 2 * side + last)
    return ("i3", 4 + 2 * int(z > 0) + side)


def lookup(buffers):
    start, total = {}, 0
    for name, count in buffers:
        start[name] = total
        total += count
    table = np.full((2, CELLS, 27), -1, np.int32)
    for parity in range(2):
        for cell in range(CELLS):
            for code in range(27):
                dx, dy, dz = code // 9 - 1, code // 3 % 3 - 1, code % 3 - 1
                inner = 1 if parity == 0 else -1
                column = "own" if dy == 0 else "i" if dy == inner else "o"
                name, at = place(column, dx, cell + dz)
                if name in start:
                    table[parity, cell, code] = start[name] + at
    return table.reshape(2, CELLS * 27), total


def split(values):
    high = values.astype(BF16)
    return high, (values - high.astype(F32)).astype(BF16)


def product(a, b):
    ah, al = split(a)
    bh, bl = split(b)
    return jnp.dot(
        jnp.concatenate([ah, ah, al], axis=1),
        jnp.concatenate([bh, bl, bh], axis=0),
        preferred_element_type=F32,
    )


def apply_kernel(counts, first, table_ref, codes_ref, tiles_ref, *rest):
    buffers, rest = rest[: len(counts)], rest[len(counts) :]
    if first:
        out_ref, window, tile, window_sem, tile_sem = rest
    else:
        before_ref, out_ref, gram_ref, window, tile, window_sem, tile_sem = rest

    def entry(at):
        return table_ref[at // SLOTS * 27 + codes_ref[at]]

    copies, start = [], 0
    for n, (count, ref) in enumerate(zip(counts, buffers)):
        copy = pltpu.make_async_copy(ref, window.at[pl.ds(start, count)], window_sem.at[n])
        copy.start()
        copies.append(copy)
        start += count

    def fetch(at):
        return pltpu.make_async_copy(tiles_ref.at[at], tile.at[at], tile_sem.at[at])

    def begin(at, carry):
        @pl.when(entry(at) >= 0)
        def _():
            fetch(at).start()

        return carry

    lax.fori_loop(0, CELLS * SLOTS, begin, 0)
    for copy in copies:
        copy.wait()
    for cell in range(CELLS):
        out_ref[cell] = -0.5 * window[cell] if first else before_ref[cell]

    def slot(at, carry):
        e = entry(at)

        @pl.when(e >= 0)
        def _():
            fetch(at).wait()
            cell = at // SLOTS
            out_ref[cell] += product(tile[at], window[e])

        return carry

    lax.fori_loop(0, CELLS * SLOTS, slot, 0)
    if not first:
        gram = jnp.zeros((SIDE, SIDE), F32)
        for cell in range(CELLS):
            high, low = split(out_ref[cell])
            gram += lax.dot_general(
                jnp.concatenate([high, high, low], axis=0),
                jnp.concatenate([high, low, high], axis=0),
                (((0,), (0,)), ((), ())),
                preferred_element_type=F32,
            )
        half = SIDE // 2
        gram_ref[:half] = gram[:half, :half]
        gram_ref[half : 2 * half] = gram[:half, half:]
        gram_ref[2 * half :] = gram[half:, half:]


def apply(names, table, codes, tiles, buffers, before=None):
    counts = tuple(count for _, count in names)
    first = before is None
    smem = pl.BlockSpec(memory_space=pltpu.SMEM)
    anywhere = pl.BlockSpec(memory_space=pl.ANY)
    vmem = pl.BlockSpec(memory_space=pltpu.VMEM)
    panel = jax.ShapeDtypeStruct((CELLS, SIDE, SIDE), F32)
    packed = jax.ShapeDtypeStruct((3 * SIDE // 2, SIDE // 2), F32)
    return pl.pallas_call(
        functools.partial(apply_kernel, counts, first),
        out_shape=panel if first else (panel, packed),
        in_specs=[smem, smem, anywhere] + [anywhere] * len(counts) + ([] if first else [vmem]),
        out_specs=vmem if first else (vmem, vmem),
        scratch_shapes=[
            pltpu.VMEM((sum(counts), SIDE, SIDE), F32),
            pltpu.VMEM((CELLS * SLOTS, SIDE, SIDE), F32),
            pltpu.SemaphoreType.DMA((len(counts),)),
            pltpu.SemaphoreType.DMA((CELLS * SLOTS,)),
        ],
        compiler_params=pltpu.CompilerParams(vmem_limit_bytes=40 << 20),
        cost_estimate=pl.CostEstimate(
            flops=(30 if first else 10) * 2 * 3 * SIDE**3, bytes_accessed=16 << 20, transcendentals=0
        ),
        name="apply_early" if first else "apply_late",
    )(table, codes, tiles, *buffers, *(() if first else (before,)))


def leaf(rows):
    rows = list(rows)
    at = lax.broadcasted_iota(jnp.int32, (8, 128), 0)
    count = len(rows)
    for b in range(count):
        rest = range(b, count)
        column = {
            (k, v): jnp.broadcast_to(rows[v][:, 8 * b + k : 8 * b + k + 1], (8, 128))
            for k in range(8)
            for v in rest
        }
        for j in range(8):
            scale = lax.rsqrt(jnp.broadcast_to(column[j, b][j : j + 1], (8, 128)))
            times = {v: column[j, v] * scale for v in rest}
            times[b] = jnp.where(at > j, times[b], 0.0)
            for k in range(j + 1, 8):
                pivot = jnp.broadcast_to(column[k, b][j : j + 1], (8, 128)) * scale
                for v in rest:
                    column[k, v] = column[k, v] - times[v] * pivot
            pivot = jnp.broadcast_to(rows[b][j : j + 1], (8, 128)) * scale
            for v in rest:
                if v > b:
                    rows[v] = rows[v] - times[v] * pivot
            rows[b] = jnp.where(at == j, pivot, rows[b] - times[b] * pivot)
    return rows


def factor_kernel(total, gram_ref, filtered_ref, bands_ref, factor_ref, work):
    half = SIDE // 2
    row = lax.broadcasted_iota(jnp.int32, (SIDE, SIDE), 0)
    col = lax.broadcasted_iota(jnp.int32, (SIDE, SIDE), 1)
    work[:half, :half] = gram_ref[:half] * (1.0 / total)
    work[:half, half:SIDE] = gram_ref[half : 2 * half] * (1.0 / total)
    work[half:, :half] = jnp.zeros((half, half), F32)
    work[half:, half:SIDE] = gram_ref[2 * half :] * (1.0 / total)
    work[:, SIDE:] = (row == col).astype(F32)
    eye = (row == col)[:BLOCK, :BLOCK].astype(F32)
    for low in range(0, SIDE, BLOCK):
        high = low + BLOCK
        rows = pl.ds(low, BLOCK)
        block = jnp.concatenate([work[rows, low:high], eye], axis=1)
        done = jnp.concatenate(leaf([block[8 * v : 8 * v + 8] for v in range(BLOCK // 8)]), axis=0)
        solved = jnp.dot(done[:, BLOCK:], work[rows, :], precision=EXACT, preferred_element_type=F32)
        work[rows, :] = solved
        if high < SIDE:
            under = pl.ds(high, SIDE - high)
            work[under, :] = work[under, :] - lax.dot_general(
                solved[:, high:SIDE],
                solved,
                (((0,), (0,)), ((), ())),
                precision=EXACT,
                preferred_element_type=F32,
            )
    factor_ref[...] = jnp.where(row <= col, work[:, :SIDE], 0.0)
    high, low = split(jnp.where(row >= col, work[:, SIDE:], 0.0))
    right = jnp.concatenate([high, low, high], axis=1)
    for cell in range(CELLS):
        fh, fl = split(filtered_ref[cell])
        bands_ref[cell] = lax.dot_general(
            jnp.concatenate([fh, fh, fl], axis=1),
            right,
            (((1,), (1,)), ((), ())),
            preferred_element_type=F32,
        )


def factorise(gram, filtered, total):
    vmem = pl.BlockSpec(memory_space=pltpu.VMEM)
    return pl.pallas_call(
        functools.partial(factor_kernel, total),
        out_shape=(
            jax.ShapeDtypeStruct((CELLS, SIDE, SIDE), F32),
            jax.ShapeDtypeStruct((SIDE, SIDE), F32),
        ),
        in_specs=[vmem, vmem],
        out_specs=(vmem, vmem),
        scratch_shapes=[pltpu.VMEM((SIDE, 2 * SIDE), F32)],
        compiler_params=pltpu.CompilerParams(vmem_limit_bytes=32 << 20),
        name="factorise",
    )(gram, filtered)


def flip(values, axis, bit):
    size = lax.axis_size(axis)
    return lax.ppermute(values, axis, [(i, i ^ bit) for i in range(size)])


def summed(values):
    halved = (("gy", 1), ("gx", 1), ("gx", 2))
    for axis, bit in halved:
        half = values.shape[0] // 2
        upper = (lax.axis_index(axis) // bit) % 2 == 1
        a, b = values[:half], values[half:]
        values = jnp.where(upper, b, a) + flip(jnp.where(upper, a, b), axis, bit)
    for axis, bit in (("gy", 2), ("gy", 4), ("gz", 1), ("gz", 2), ("gz", 4)):
        values = values + flip(values, axis, bit)
    for axis, bit in halved[::-1]:
        upper = (lax.axis_index(axis) // bit) % 2 == 1
        other = flip(values, axis, bit)
        values = jnp.concatenate(
            [jnp.where(upper, other, values), jnp.where(upper, values, other)], axis=0
        )
    return values


def up(values, axis):
    return lax.ppermute(values, axis, [(i, i + 1) for i in range(lax.axis_size(axis) - 1)])


def down(values, axis):
    return lax.ppermute(values, axis, [(i + 1, i) for i in range(lax.axis_size(axis) - 1)])


def across(values):
    size = lax.axis_size("gy")
    pairs = [(i, i + 1) for i in range(1, size - 1, 2)]
    return lax.ppermute(values, "gy", pairs + [(j, i) for i, j in pairs])


def per_device(panel, tiles, codes):
    own = panel[0, 0]
    ends = jnp.concatenate([own[:1], own[CELLS - 1 :]], axis=0)
    mids = own[1:3]
    got = {"own": own}
    got["ends-"], got["ends+"] = up(ends, "gx"), down(ends, "gx")
    got["o"] = across(own)
    got["below"], got["above"] = up(own[CELLS - 1 :], "gz"), down(own[:1], "gz")
    got["i"] = flip(own, "gy", 1)

    sides = jnp.concatenate([got["ends-"], got["ends+"]], axis=0)
    got["o_ends"] = across(sides)
    tops = jnp.concatenate([sides[1:2], sides[3:], got["o"][CELLS - 1 :]], axis=0)
    bottoms = jnp.concatenate([sides[:1], sides[2:3], got["o"][:1]], axis=0)
    got["below2"], got["above2"] = up(tops, "gz"), down(bottoms, "gz")
    got["mids-"], got["mids+"] = up(mids, "gx"), down(mids, "gx")
    got["i2"] = flip(jnp.concatenate([sides, got["below"], got["above"]], axis=0), "gy", 1)

    middle = jnp.concatenate([got["mids-"], got["mids+"]], axis=0)
    got["o_mids"] = across(middle)
    o_ends = got["o_ends"]
    got["below3"] = up(jnp.concatenate([o_ends[1:2], o_ends[3:]], axis=0), "gz")
    got["above3"] = down(jnp.concatenate([o_ends[:1], o_ends[2:3]], axis=0), "gz")
    got["i3"] = flip(
        jnp.concatenate([middle, got["below2"][:2], got["above2"][:2]], axis=0), "gy", 1
    )

    odd = lax.axis_index("gy") % 2 == 1
    flat_tiles = tiles.reshape(CELLS * SLOTS, SIDE, SIDE)
    flat_codes = codes.reshape(CELLS * SLOTS)
    filtered = None
    for names in (EARLY, LATE):
        table, _ = lookup(names)
        chosen = jnp.where(odd, jnp.asarray(table[1]), jnp.asarray(table[0]))
        filtered = apply(
            names, chosen, flat_codes, flat_tiles, [got[name] for name, _ in names], filtered
        )
    filtered, gram = filtered
    devices = lax.axis_size("gx") * lax.axis_size("gy") * lax.axis_size("gz")
    bands, factor = factorise(summed(gram), filtered, CELLS * SIDE * devices)
    return bands.reshape(panel.shape), factor


def solution(mesh):
    in_specs = (
        P("gx", "gy", "gz", None, None),
        P("gx", "gy", "gz", None, None, None),
        P("gx", "gy", "gz", None),
    )
    out_specs = (P("gx", "gy", "gz", None, None), P())
    return jax.shard_map(
        per_device, mesh=mesh, in_specs=in_specs, out_specs=out_specs, check_vma=False
    )
```

time: 536 us -> 168 us (0.31)
  waiting for transfers between devices: 358 us -> 46.8 us
  other arithmetic: 68.5 us -> 5.92 us
  starting transfers between devices: 18.7 us -> 72 us
  matrix products: 31.6 us -> 0 us
  Pallas kernels: 0 us -> 30.9 us
  local copies, waits for them, and re-layouts: 39.6 us -> 10.2 us
  between operations: 15.8 us -> 1.09 us
    psum x1 -> x0, waiting for transfers between devices: 274 us -> none  [per_device(): summed = lax.psum(local_gram, ('gx', 'gy', 'gz'))]
    another operation x8 -> x0, other arithmetic: 53.8 us -> none  [the longest x6 34.1 us: per_device(): lower = jnp.linalg.cholesky(gram)]
    ppermute x6 -> x27, starting transfers between devices: 18.7 us -> 72 us  [the longest x14 33.5 us: flip(): return lax.ppermute(values, axis, [(i, i ^ bit) for i in range(size)])]
    ppermute x6 -> x27, waiting for transfers between devices: 83.5 us -> 46.8 us  [the longest x14 18 us: flip(): return lax.ppermute(values, axis, [(i, i ^ bit) for i in range(size)])]
    pallas_call x0 -> x3, Pallas kernels: none -> 30.9 us  [the longest x2 19.7 us: apply(): pl.pallas_call(functools.partial(apply_kernel, counts, first), out_shape=...]
    dot_general x6 -> x0, matrix products: 30.3 us -> none  [the longest x4 25.7 us: per_device(): jnp.einsum('kab,kbc->ac', tiles[0, 0, element_cell], windows, precision=l...]
    gather x4 -> x0, local copies, waits for them, and re-layouts: 27.8 us -> none  [window(): lax.dynamic_slice(padded, (first, second, third, zero, zero), (1, 1, 1, p...]
  transfers between devices with their start and end apart: 7 -> 27, of which waited for: 7 -> 16; matrix products, arithmetic and copies ran while one was open for 1% -> 4% of each run, Pallas kernels for 0% -> 7%
where the time goes in v1:
time: 168 us; the launch traced here: 167 us
  starting transfers between devices  72 us (43%)
  waiting for transfers between devices  46.8 us (28%)
  Pallas kernels  30.9 us (18%)
  local copies, waits for them, and re-layouts  10.2 us (6%)
  other arithmetic  5.92 us (4%)
    ppermute x14, starting transfers between devices, flip(): return lax.ppermute(values, axis, [(i, i ^ bit) for i in range(size)])  33.5 us
    pallas_call x2, Pallas kernels, apply(): pl.pallas_call(functools.partial(apply_kernel, counts, first), out_shape=...  19.7 us
    ppermute x5, starting transfers between devices, up(): lax.ppermute(values, axis, [(i, i + 1) for i in range(lax.axis_size(axis)...  19.1 us
    ppermute x14, waiting for transfers between devices, flip(): return lax.ppermute(values, axis, [(i, i ^ bit) for i in range(size)])  18 us
    ppermute x5, waiting for transfers between devices, up(): lax.ppermute(values, axis, [(i, i + 1) for i in range(lax.axis_size(axis)...  15.7 us
    ppermute x3, starting transfers between devices, across(): return lax.ppermute(values, 'gy', pairs + [(j, i) for i, j in pairs])  13 us
    pallas_call x1, Pallas kernels, factorise(): pl.pallas_call(functools.partial(factor_kernel, total), out_shape=(jax.Sh...  11.2 us
    unnamed x36, local copies, waits for them, and re-layouts  8.73 us
  transfers between devices with their start and end apart: 27, of which 16 were waited for; matrix products, arithmetic and copies ran while one was open for 4% of the time, Pallas kernels for 7%

profile of v1, /device:TPU:1, one launch (start us, length us, event | category | flops | bytes accessed | tf_op | source)
XLA Modules:
  0.0 166.9 jit_solution(8866784187274358033)
XLA Ops:
  0.6 4.6 %collective-permute-start.8 = (f32[4,256,256]{2,1,0:T(8,128)}, f32[4,256,256]{2,1,0:T(8,128)S(1)}, u32[]{:S(2)}, u32[]{:S(2)}) collective-permute-start(f32[4,256,256]{2,1,0:T(8,128)} %bitcast.9), channel_id=1, source_target_pairs={{8,16},{24,32},{40,48},{16,8},{32,24},{48,40},{9,17},{25,33},{41,4... | collective-permute-start | bytes 3145736 | tf_op jit(solution)/shard_map/ppermute | solution.py:289
  5.2 1.1 slice_bitcast_fusion.2
  6.3 3.1 %collective-permute-start.3 = (f32[2,256,256]{2,1,0:T(8,128)S(1)}, f32[2,256,256]{2,1,0:T(8,128)S(1)}, u32[]{:S(2)}, u32[]{:S(2)}) collective-permute-start(f32[2,256,256]{2,1,0:T(8,128)S(1)} %pad_maximum_fusion.6), channel_id=1, source_target_pairs={{0,64},{64,128},{128,192},{1,65},{65,129},{129,193},{2,66},{66,130... | collective-permute-start | bytes 1572872 | tf_op jit(solution)/shard_map/ppermute | solution.py:279
  9.5 1.3 collective-permute-start.4
  10.8 8.5 %collective-permute-done.3.rest_5_ = f32[2,256,256]{2,1,0:T(8,128)S(1)} collective-permute-done((f32[2,256,256]{2,1,0:T(8,128)S(1)}, f32[2,256,256]{2,1,0:T(8,128)S(1)}, u32[]{:S(2)}, u32[]{:S(2)}) %collective-permute-start.3) | collective-permute-done | bytes 524320 | tf_op jit(solution)/shard_map/ppermute | solution.py:279
  19.3 4.1 %collective-permute-done.4.rest_6_ = f32[2,256,256]{2,1,0:T(8,128)S(1)} collective-permute-done((f32[2,256,256]{2,1,0:T(8,128)S(1)}, f32[2,256,256]{2,1,0:T(8,128)S(1)}, u32[]{:S(2)}, u32[]{:S(2)}) %collective-permute-start.4) | collective-permute-done | bytes 524320 | tf_op jit(solution)/shard_map/ppermute | solution.py:283
  23.5 0.1 pad_maximum_fusion.4
  23.6 3.7 %collective-permute-start.9 = (f32[3,256,256]{2,1,0:T(8,128)S(1)}, f32[3,256,256]{2,1,0:T(8,128)S(1)}, u32[]{:S(2)}, u32[]{:S(2)}) collective-permute-start(f32[3,256,256]{2,1,0:T(8,128)S(1)} %pad_maximum_fusion.4), channel_id=1, source_target_pairs={{0,1},{1,2},{2,3},{3,4},{4,5},{5,6},{6,7},{8,9},{9,10},{10,11},{11... | collective-permute-start | bytes 2359304 | tf_op jit(solution)/shard_map/ppermute | solution.py:279
  27.3 0.1 pad_maximum_fusion.5
  27.4 1.3 collective-permute-start.10
  28.8 3.1 %collective-permute-start = (f32[2,256,256]{2,1,0:T(8,128)S(1)}, f32[2,256,256]{2,1,0:T(8,128)S(1)}, u32[]{:S(2)}, u32[]{:S(2)}) collective-permute-start(f32[2,256,256]{2,1,0:T(8,128)S(1)} %slice_bitcast_fusion), channel_id=1, source_target_pairs={{0,64},{64,128},{128,192},{1,65},{65,129},{129,193},{2,66},{66,130... | collective-permute-start | bytes 1572872 | tf_op jit(solution)/shard_map/ppermute | solution.py:279
  31.9 1.3 collective-permute-start.1
  33.2 4.1 %collective-permute-start.13 = (f32[1,256,256]{2,1,0:T(8,128)S(1)}, f32[1,256,256]{2,1,0:T(8,128)S(1)}, u32[]{:S(2)}, u32[]{:S(2)}) collective-permute-start(f32[1,256,256]{2,1,0:T(8,128)S(1)} %get-tuple-element.17), channel_id=1, source_target_pairs={{0,1},{1,2},{2,3},{3,4},{4,5},{5,6},{6,7},{8,9},{9,10},{10,11},{11... | collective-permute-start | bytes 786440 | tf_op jit(solution)/shard_map/ppermute | solution.py:279
  37.3 7.2 %collective-permute-done.9.rest_10_ = f32[3,256,256]{2,1,0:T(8,128)S(1)} collective-permute-done((f32[3,256,256]{2,1,0:T(8,128)S(1)}, f32[3,256,256]{2,1,0:T(8,128)S(1)}, u32[]{:S(2)}, u32[]{:S(2)}) %collective-permute-start.9) | collective-permute-done | bytes 786464 | tf_op jit(solution)/shard_map/ppermute | solution.py:279
  44.6 1.3 collective-permute-start.14
  45.9 2.4 %collective-permute-done.10.rest_11_ = f32[3,256,256]{2,1,0:T(8,128)S(1)} collective-permute-done((f32[3,256,256]{2,1,0:T(8,128)S(1)}, f32[3,256,256]{2,1,0:T(8,128)S(1)}, u32[]{:S(2)}, u32[]{:S(2)}) %collective-permute-start.10) | collective-permute-done | bytes 786464 | tf_op jit(solution)/shard_map/ppermute | solution.py:283
  48.4 0.8 copy-done.7
  49.2 1.5 pad_maximum_fusion
  50.7 0.4 collective-permute-start.11
  51.1 0.1 pad_maximum_fusion.3
  51.2 5.0 %collective-permute-start.5 = (f32[4,256,256]{2,1,0:T(8,128)S(1)}, f32[4,256,256]{2,1,0:T(8,128)S(1)}, u32[]{:S(2)}, u32[]{:S(2)}) collective-permute-start(f32[4,256,256]{2,1,0:T(8,128)S(1)} %pad_maximum_fusion.3), channel_id=1, source_target_pairs={{8,16},{24,32},{40,48},{16,8},{32,24},{48,40},{9,17},{25,33},{41,4... | collective-permute-start | bytes 3145736 | tf_op jit(solution)/shard_map/ppermute | solution.py:289
  56.2 1.2 pad_maximum_fusion.1
  57.5 0.5 collective-permute-start.12
  58.0 1.0 pad_maximum_fusion.2
  59.0 3.4 %collective-permute-start.2 = (f32[4,256,256]{2,1,0:T(8,128)}, f32[4,256,256]{2,1,0:T(8,128)}, u32[]{:S(2)}, u32[]{:S(2)}) collective-permute-start(f32[4,256,256]{2,1,0:T(8,128)} %pad_maximum_fusion.2), channel_id=1, source_target_pairs={{8,16},{24,32},{40,48},{16,8},{32,24},{48,40},{9,17},{25,33},{41,4... | collective-permute-start | bytes 3145736 | tf_op jit(solution)/shard_map/ppermute | solution.py:289
  62.5 6.6 %collective-permute-done.5.rest_9_ = f32[4,256,256]{2,1,0:T(8,128)S(1)} collective-permute-done((f32[4,256,256]{2,1,0:T(8,128)S(1)}, f32[4,256,256]{2,1,0:T(8,128)S(1)}, u32[]{:S(2)}, u32[]{:S(2)}) %collective-permute-start.5) | collective-permute-done | bytes 1048608 | tf_op jit(solution)/shard_map/ppermute | solution.py:289
  69.0 0.1 fusion.1
  69.1 0.9 pad_maximum_fusion.8
  70.0 1.3 collective-permute-start.7
  71.3 0.8 pad_maximum_fusion.7
  72.2 1.0 copy-done.11
  73.1 5.0 %collective-permute-start.6 = (f32[2,256,256]{2,1,0:T(8,128)}, f32[2,256,256]{2,1,0:T(8,128)}, u32[]{:S(2)}, u32[]{:S(2)}) collective-permute-start(f32[2,256,256]{2,1,0:T(8,128)} %pad_maximum_fusion.7), channel_id=1, source_target_pairs={{0,1},{1,2},{2,3},{3,4},{4,5},{5,6},{6,7},{8,9},{9,10},{10,11},{11... | collective-permute-start | bytes 1572872 | tf_op jit(solution)/shard_map/ppermute | solution.py:279
  78.1 0.1 reshape.16.codes_ref
  78.3 1.2 copy-done.2
  79.5 1.2 copy-done.4
  80.7 1.1 copy-done.6
  81.9 1.1 copy-done.8
  83.0 0.9 copy-done.10
  83.9 1.2 copy-done.12
  85.2 12.2 %apply_early.1.rest_4_ = f32[4,256,256]{2,1,0:T(8,128)S(1)} custom-call(s32[108]{0:T(128)S(1)} %get-tuple-element.28.table_ref, s32[40]{0:T(128)S(1)} %reshape.16.codes_ref, f32[40,256,256]{2,1,0:T(8,128)} %bitcast.12, f32[4,256,256]{2,1,0:T(8,128)S(1)} %bitcast.11, f32[4,256,256]{2,1,0:T(8,128)S(1)} %copy-done.4, f32[4,256,256]{2,1,0:T(8,128)S(1)} %copy-done.12, ...), custom_call_target="tpu_custom_call" | custom-call | flops 3019898880 | bytes 16777216 | tf_op jit(solution)/shard_map/apply_early/pallas_call | solution.py:154
  97.4 7.5 %apply_late.1 = (f32[4,256,256]{2,1,0:T(8,128)S(1)}, f32[384,128]{1,0:T(8,128)S(1)}) custom-call(s32[108]{0:T(128)S(1)} %get-tuple-element.29.table_ref, s32[40]{0:T(128)S(1)} %reshape.16.codes_ref, f32[40,256,256]{2,1,0:T(8,128)} %bitcast.13, f32[4,256,256]{2,1,0:T(8,128)} %collective-permute-done.2.rest_0_, f32[2,256,256]{2,1,0:T(8,128)} %collective-permute-done.6.rest_1_, ...), custom_call_target="tpu_custom_call" | custom-call | flops 1006632960 | bytes 16777216 | tf_op jit(solution)/shard_map/apply_late/pallas_call | solution.py:154
  105.0 0.1 collective-permute-start.16
  105.1 1.3 collective-permute-done.16
  106.4 1.3 collective-permute-start.17
  107.7 1.8 %collective-permute-done.17 = f32[96,128]{1,0:T(8,128)S(1)} collective-permute-done((f32[96,128]{1,0:T(8,128)S(1)}, f32[96,128]{1,0:T(8,128)S(1)}, u32[]{:S(2)}, u32[]{:S(2)}) %collective-permute-start.17) | collective-permute-done | bytes 49184 | tf_op jit(solution)/shard_map/ppermute | solution.py:257
  109.4 2.5 %collective-permute-start.18 = (f32[48,128]{1,0:T(8,128)S(1)}, f32[48,128]{1,0:T(8,128)S(1)}, u32[]{:S(2)}, u32[]{:S(2)}) collective-permute-start(f32[48,128]{1,0:T(8,128)S(1)} %slice_select_fusion.2), channel_id=1, source_target_pairs={{0,128},{64,192},{128,0},{192,64},{1,129},{65,193},{129,1},{193,65... | collective-permute-start | bytes 73736 | tf_op jit(solution)/shard_map/ppermute | solution.py:257
  111.9 1.8 %collective-permute-done.18 = f32[48,128]{1,0:T(8,128)S(1)} collective-permute-done((f32[48,128]{1,0:T(8,128)S(1)}, f32[48,128]{1,0:T(8,128)S(1)}, u32[]{:S(2)}, u32[]{:S(2)}) %collective-permute-start.18) | collective-permute-done | bytes 24608 | tf_op jit(solution)/shard_map/ppermute | solution.py:257
  113.7 1.9 %collective-permute-start.19 = (f32[48,128]{1,0:T(8,128)S(1)}, f32[48,128]{1,0:T(8,128)S(1)}, u32[]{:S(2)}, u32[]{:S(2)}) collective-permute-start(f32[48,128]{1,0:T(8,128)S(1)} %select_add_fusion.2), channel_id=1, source_target_pairs={{0,16},{8,24},{16,0},{24,8},{32,48},{40,56},{48,32},{56,40},{1,17}... | collective-permute-start | bytes 73736 | tf_op jit(solution)/shard_map/ppermute | solution.py:257
  115.6 1.2 collective-permute-done.19
  116.8 3.2 %collective-permute-start.20 = (f32[48,128]{1,0:T(8,128)S(1)}, f32[48,128]{1,0:T(8,128)S(1)}, u32[]{:S(2)}, u32[]{:S(2)}) collective-permute-start(f32[48,128]{1,0:T(8,128)S(1)} %add.47), channel_id=1, source_target_pairs={{0,32},{8,40},{16,48},{24,56},{32,0},{40,8},{48,16},{56,24},{1,33}... | collective-permute-start | bytes 73736 | tf_op jit(solution)/shard_map/ppermute | solution.py:257
  120.0 1.3 collective-permute-done.20
  121.3 2.5 %collective-permute-start.21 = (f32[48,128]{1,0:T(8,128)S(1)}, f32[48,128]{1,0:T(8,128)S(1)}, u32[]{:S(2)}, u32[]{:S(2)}) collective-permute-start(f32[48,128]{1,0:T(8,128)S(1)} %add.48), channel_id=1, source_target_pairs={{0,1},{1,0},{2,3},{3,2},{4,5},{5,4},{6,7},{7,6},{8,9},{9,8},{10,11... | collective-permute-start | bytes 73736 | tf_op jit(solution)/shard_map/ppermute | solution.py:257
  123.8 1.5 collective-permute-done.21
  125.3 4.5 %collective-permute-start.22 = (f32[48,128]{1,0:T(8,128)S(1)}, f32[48,128]{1,0:T(8,128)S(1)}, u32[]{:S(2)}, u32[]{:S(2)}) collective-permute-start(f32[48,128]{1,0:T(8,128)S(1)} %add.49), channel_id=1, source_target_pairs={{0,2},{1,3},{2,0},{3,1},{4,6},{5,7},{6,4},{7,5},{8,10},{9,11},{10,... | collective-permute-start | bytes 73736 | tf_op jit(solution)/shard_map/ppermute | solution.py:257
  129.8 1.2 collective-permute-done.22
  131.1 3.1 %collective-permute-start.23 = (f32[48,128]{1,0:T(8,128)S(1)}, f32[48,128]{1,0:T(8,128)S(1)}, u32[]{:S(2)}, u32[]{:S(2)}) collective-permute-start(f32[48,128]{1,0:T(8,128)S(1)} %add.50), channel_id=1, source_target_pairs={{0,4},{1,5},{2,6},{3,7},{4,0},{5,1},{6,2},{7,3},{8,12},{9,13},{10,... | collective-permute-start | bytes 73736 | tf_op jit(solution)/shard_map/ppermute | solution.py:257
  134.2 3.4 %collective-permute-done.23 = f32[48,128]{1,0:T(8,128)S(1)} collective-permute-done((f32[48,128]{1,0:T(8,128)S(1)}, f32[48,128]{1,0:T(8,128)S(1)}, u32[]{:S(2)}, u32[]{:S(2)}) %collective-permute-start.23) | collective-permute-done | bytes 24608 | tf_op jit(solution)/shard_map/ppermute | solution.py:257
  137.7 2.4 %collective-permute-start.24 = (f32[48,128]{1,0:T(8,128)S(1)}, f32[48,128]{1,0:T(8,128)S(1)}, u32[]{:S(2)}, u32[]{:S(2)}) collective-permute-start(f32[48,128]{1,0:T(8,128)S(1)} %add.51), channel_id=1, source_target_pairs={{0,128},{64,192},{128,0},{192,64},{1,129},{65,193},{129,1},{193,65... | collective-permute-start | bytes 73736 | tf_op jit(solution)/shard_map/ppermute | solution.py:257
  140.1 1.8 %collective-permute-done.24 = f32[48,128]{1,0:T(8,128)S(1)} collective-permute-done((f32[48,128]{1,0:T(8,128)S(1)}, f32[48,128]{1,0:T(8,128)S(1)}, u32[]{:S(2)}, u32[]{:S(2)}) %collective-permute-start.24) | collective-permute-done | bytes 24608 | tf_op jit(solution)/shard_map/ppermute | solution.py:257
  141.9 1.3 collective-permute-start.25
  143.1 1.8 %collective-permute-done.25 = f32[96,128]{1,0:T(8,128)S(1)} collective-permute-done((f32[96,128]{1,0:T(8,128)S(1)}, f32[96,128]{1,0:T(8,128)S(1)}, u32[]{:S(2)}, u32[]{:S(2)}) %collective-permute-start.25) | collective-permute-done | bytes 49184 | tf_op jit(solution)/shard_map/ppermute | solution.py:257
  144.9 9.8 %collective-permute-start.26 = (f32[192,128]{1,0:T(8,128)S(1)}, f32[192,128]{1,0:T(8,128)S(1)}, u32[]{:S(2)}, u32[]{:S(2)}) collective-permute-start(f32[192,128]{1,0:T(8,128)S(1)} %pad_maximum_fusion.10), channel_id=1, source_target_pairs={{0,8},{8,0},{16,24},{24,16},{32,40},{40,32},{48,56},{56,48},{1,9},... | collective-permute-start | bytes 294920 | tf_op jit(solution)/shard_map/ppermute | solution.py:257
  154.7 0.9 collective-permute-done.26
  155.7 11.2 %factorise.1 = (f32[4,256,256]{2,1,0:T(8,128)}, f32[256,256]{1,0:T(8,128)}) custom-call(f32[384,128]{1,0:T(8,128)S(1)} %pad_maximum_fusion.9.gram_ref, f32[4,256,256]{2,1,0:T(8,128)S(1)} %get-tuple-element.7.filtered_ref), custom_call_target="tpu_custom_call" | custom-call | tf_op jit(solution)/shard_map/factorise/pallas_call | solution.py:241
  (65 shorter events, 0.5 us)
Async XLA Ops:
  0.6 22.8 %collective-permute-start.8 = (f32[4,256,256]{2,1,0:T(8,128)}, f32[4,256,256]{2,1,0:T(8,128)S(1)}, u32[]{:S(2)}, u32[]{:S(2)}) collective-permute-start(f32[4,256,256]{2,1,0:T(8,128)} %bitcast.9), channel_id=1, source_target_pairs={{8,16},{24,32},{40,48},{16,8},{32,24},{48,40},{9,17},{25,33},{41,4... | collective-permute-start | bytes 3145736 | tf_op jit(solution)/shard_map/ppermute | solution.py:289
  6.3 12.9 %collective-permute-start.3 = (f32[2,256,256]{2,1,0:T(8,128)S(1)}, f32[2,256,256]{2,1,0:T(8,128)S(1)}, u32[]{:S(2)}, u32[]{:S(2)}) collective-permute-start(f32[2,256,256]{2,1,0:T(8,128)S(1)} %pad_maximum_fusion.6), channel_id=1, source_target_pairs={{0,64},{64,128},{128,192},{1,65},{65,129},{129,193},{2,66},{66,130... | collective-permute-start | bytes 1572872 | tf_op jit(solution)/shard_map/ppermute | solution.py:279
  9.5 13.9 %collective-permute-start.4 = (f32[2,256,256]{2,1,0:T(8,128)S(1)}, f32[2,256,256]{2,1,0:T(8,128)S(1)}, u32[]{:S(2)}, u32[]{:S(2)}) collective-permute-start(f32[2,256,256]{2,1,0:T(8,128)S(1)} %pad_maximum_fusion.6), channel_id=1, source_target_pairs={{64,0},{128,64},{192,128},{65,1},{129,65},{193,129},{66,2},{130,66... | collective-permute-start | bytes 1572872 | tf_op jit(solution)/shard_map/ppermute | solution.py:283
  23.5 5.2 %copy-start = (f32[1,1,4,256,256]{4,3,2,1,0:T(8,128)S(1)}, f32[1,1,4,256,256]{4,3,2,1,0:T(8,128)}, u32[]{:S(2)}) copy-start(f32[1,1,4,256,256]{4,3,2,1,0:T(8,128)} %param.7) | copy-start | bytes 3145732
  23.5 3.9 %copy-start.3 = (f32[4,256,256]{2,1,0:T(8,128)}, f32[4,256,256]{2,1,0:T(8,128)S(1)}, u32[]{:S(2)}) copy-start(f32[4,256,256]{2,1,0:T(8,128)S(1)} %collective-permute-done.8.rest_1_) | copy-start | bytes 3145732
  23.6 21.0 %collective-permute-start.9 = (f32[3,256,256]{2,1,0:T(8,128)S(1)}, f32[3,256,256]{2,1,0:T(8,128)S(1)}, u32[]{:S(2)}, u32[]{:S(2)}) collective-permute-start(f32[3,256,256]{2,1,0:T(8,128)S(1)} %pad_maximum_fusion.4), channel_id=1, source_target_pairs={{0,1},{1,2},{2,3},{3,4},{4,5},{5,6},{6,7},{8,9},{9,10},{10,11},{11... | collective-permute-start | bytes 2359304 | tf_op jit(solution)/shard_map/ppermute | solution.py:279
  27.4 20.9 %collective-permute-start.10 = (f32[3,256,256]{2,1,0:T(8,128)S(1)}, f32[3,256,256]{2,1,0:T(8,128)S(1)}, u32[]{:S(2)}, u32[]{:S(2)}) collective-permute-start(f32[3,256,256]{2,1,0:T(8,128)S(1)} %pad_maximum_fusion.5), channel_id=1, source_target_pairs={{1,0},{2,1},{3,2},{4,3},{5,4},{6,5},{7,6},{9,8},{10,9},{11,10},{12... | collective-permute-start | bytes 2359304 | tf_op jit(solution)/shard_map/ppermute | solution.py:283
  28.8 19.6 %collective-permute-start = (f32[2,256,256]{2,1,0:T(8,128)S(1)}, f32[2,256,256]{2,1,0:T(8,128)S(1)}, u32[]{:S(2)}, u32[]{:S(2)}) collective-permute-start(f32[2,256,256]{2,1,0:T(8,128)S(1)} %slice_bitcast_fusion), channel_id=1, source_target_pairs={{0,64},{64,128},{128,192},{1,65},{65,129},{129,193},{2,66},{66,130... | collective-permute-start | bytes 1572872 | tf_op jit(solution)/shard_map/ppermute | solution.py:279
  31.9 17.3 %collective-permute-start.1 = (f32[2,256,256]{2,1,0:T(8,128)S(1)}, f32[2,256,256]{2,1,0:T(8,128)S(1)}, u32[]{:S(2)}, u32[]{:S(2)}) collective-permute-start(f32[2,256,256]{2,1,0:T(8,128)S(1)} %slice_bitcast_fusion), channel_id=1, source_target_pairs={{64,0},{128,64},{192,128},{65,1},{129,65},{193,129},{66,2},{130,66... | collective-permute-start | bytes 1572872 | tf_op jit(solution)/shard_map/ppermute | solution.py:283
  33.2 23.0 %collective-permute-start.13 = (f32[1,256,256]{2,1,0:T(8,128)S(1)}, f32[1,256,256]{2,1,0:T(8,128)S(1)}, u32[]{:S(2)}, u32[]{:S(2)}) collective-permute-start(f32[1,256,256]{2,1,0:T(8,128)S(1)} %get-tuple-element.17), channel_id=1, source_target_pairs={{0,1},{1,2},{2,3},{3,4},{4,5},{5,6},{6,7},{8,9},{9,10},{10,11},{11... | collective-permute-start | bytes 786440 | tf_op jit(solution)/shard_map/ppermute | solution.py:279
  44.6 3.8 %copy-start.5 = (f32[3,256,256]{2,1,0:T(8,128)}, f32[3,256,256]{2,1,0:T(8,128)S(1)}, u32[]{:S(2)}) copy-start(f32[3,256,256]{2,1,0:T(8,128)S(1)} %collective-permute-done.9.rest_10_) | copy-start | bytes 2359300
  44.6 11.6 %collective-permute-start.14 = (f32[1,256,256]{2,1,0:T(8,128)S(1)}, f32[1,256,256]{2,1,0:T(8,128)S(1)}, u32[]{:S(2)}, u32[]{:S(2)}) collective-permute-start(f32[1,256,256]{2,1,0:T(8,128)S(1)} %get-tuple-element.16), channel_id=1, source_target_pairs={{1,0},{2,1},{3,2},{4,3},{5,4},{6,5},{7,6},{9,8},{10,9},{11,10},{12... | collective-permute-start | bytes 786440 | tf_op jit(solution)/shard_map/ppermute | solution.py:283
  48.3 0.9 copy-start.7
  50.7 46.7 %collective-permute-start.11 = (f32[8,256,256]{2,1,0:T(8,128)}, f32[8,256,256]{2,1,0:T(8,128)}, u32[]{:S(2)}, u32[]{:S(2)}) collective-permute-start(f32[8,256,256]{2,1,0:T(8,128)} %pad_maximum_fusion), channel_id=1, source_target_pairs={{0,8},{8,0},{16,24},{24,16},{32,40},{40,32},{48,56},{56,48},{1,9},... | collective-permute-start | bytes 6291464 | tf_op jit(solution)/shard_map/ppermute | solution.py:257
  51.2 17.9 %collective-permute-start.5 = (f32[4,256,256]{2,1,0:T(8,128)S(1)}, f32[4,256,256]{2,1,0:T(8,128)S(1)}, u32[]{:S(2)}, u32[]{:S(2)}) collective-permute-start(f32[4,256,256]{2,1,0:T(8,128)S(1)} %pad_maximum_fusion.3), channel_id=1, source_target_pairs={{8,16},{24,32},{40,48},{16,8},{32,24},{48,40},{9,17},{25,33},{41,4... | collective-permute-start | bytes 3145736 | tf_op jit(solution)/shard_map/ppermute | solution.py:289
  56.2 2.8 %copy-start.9 = (f32[1,256,256]{2,1,0:T(8,128)}, f32[1,256,256]{2,1,0:T(8,128)S(1)}, u32[]{:S(2)}) copy-start(f32[1,256,256]{2,1,0:T(8,128)S(1)} %collective-permute-done.14.rest_4_) | copy-start | bytes 786436
  57.5 20.8 %collective-permute-start.15 = (f32[6,256,256]{2,1,0:T(8,128)}, f32[6,256,256]{2,1,0:T(8,128)}, u32[]{:S(2)}, u32[]{:S(2)}) collective-permute-start(f32[6,256,256]{2,1,0:T(8,128)} %pad_maximum_fusion.1), channel_id=1, source_target_pairs={{0,8},{8,0},{16,24},{24,16},{32,40},{40,32},{48,56},{56,48},{1,9},... | collective-permute-start | bytes 4718600 | tf_op jit(solution)/shard_map/ppermute | solution.py:257
  57.5 14.7 %collective-permute-start.12 = (f32[4,256,256]{2,1,0:T(8,128)S(1)}, f32[4,256,256]{2,1,0:T(8,128)S(1)}, u32[]{:S(2)}, u32[]{:S(2)}) collective-permute-start(f32[4,256,256]{2,1,0:T(8,128)S(1)} %bitcast.10), channel_id=1, source_target_pairs={{0,8},{8,0},{16,24},{24,16},{32,40},{40,32},{48,56},{56,48},{1,9},... | collective-permute-start | bytes 3145736 | tf_op jit(solution)/shard_map/ppermute | solution.py:257
  59.0 19.1 %copy-start.13 = (s32[1,1,4,10]{3,2,1,0:T(4,128)S(1)}, s32[1,1,4,10]{3,2,1,0:T(4,128)}, u32[]{:S(2)}) copy-start(s32[1,1,4,10]{3,2,1,0:T(4,128)} %param.9) | copy-start | bytes 484
  59.0 19.2 %copy-start.14 = (s32[108]{0:T(128)S(1)}, s32[108]{0:T(128)}, u32[]{:S(2)}) copy-start(s32[108]{0:T(128)} %constant.82.clone) | copy-start | bytes 1300
  59.0 19.2 %copy-start.15 = (s32[108]{0:T(128)S(1)}, s32[108]{0:T(128)}, u32[]{:S(2)}) copy-start(s32[108]{0:T(128)} %constant.83.clone) | copy-start | bytes 1300
  59.0 19.2 %copy-start.16 = (s32[108]{0:T(128)S(1)}, s32[108]{0:T(128)}, u32[]{:S(2)}) copy-start(s32[108]{0:T(128)} %constant.84.clone) | copy-start | bytes 1300
  59.0 19.2 %copy-start.17 = (s32[108]{0:T(128)S(1)}, s32[108]{0:T(128)}, u32[]{:S(2)}) copy-start(s32[108]{0:T(128)} %constant.85.clone) | copy-start | bytes 1300
  59.0 38.3 %collective-permute-start.2 = (f32[4,256,256]{2,1,0:T(8,128)}, f32[4,256,256]{2,1,0:T(8,128)}, u32[]{:S(2)}, u32[]{:S(2)}) collective-permute-start(f32[4,256,256]{2,1,0:T(8,128)} %pad_maximum_fusion.2), channel_id=1, source_target_pairs={{8,16},{24,32},{40,48},{16,8},{32,24},{48,40},{9,17},{25,33},{41,4... | collective-permute-start | bytes 3145736 | tf_op jit(solution)/shard_map/ppermute | solution.py:289
  69.0 3.1 %copy-start.1 = (f32[4,256,256]{2,1,0:T(8,128)}, f32[4,256,256]{2,1,0:T(8,128)S(1)}, u32[]{:S(2)}) copy-start(f32[4,256,256]{2,1,0:T(8,128)S(1)} %collective-permute-done.5.rest_9_) | copy-start | bytes 3145732
  70.0 27.3 %collective-permute-start.7 = (f32[2,256,256]{2,1,0:T(8,128)}, f32[2,256,256]{2,1,0:T(8,128)}, u32[]{:S(2)}, u32[]{:S(2)}) collective-permute-start(f32[2,256,256]{2,1,0:T(8,128)} %pad_maximum_fusion.8), channel_id=1, source_target_pairs={{1,0},{2,1},{3,2},{4,3},{5,4},{6,5},{7,6},{9,8},{10,9},{11,10},{12... | collective-permute-start | bytes 1572872 | tf_op jit(solution)/shard_map/ppermute | solution.py:283
  72.2 1.0 copy-start.11
  73.1 24.2 %collective-permute-start.6 = (f32[2,256,256]{2,1,0:T(8,128)}, f32[2,256,256]{2,1,0:T(8,128)}, u32[]{:S(2)}, u32[]{:S(2)}) collective-permute-start(f32[2,256,256]{2,1,0:T(8,128)} %pad_maximum_fusion.7), channel_id=1, source_target_pairs={{0,1},{1,2},{2,3},{3,4},{4,5},{5,6},{6,7},{8,9},{9,10},{10,11},{11... | collective-permute-start | bytes 1572872 | tf_op jit(solution)/shard_map/ppermute | solution.py:279
  78.3 1.2 copy-start.2
  79.5 1.2 copy-start.4
  80.7 1.1 copy-start.6
  81.8 1.1 copy-start.8
  83.0 0.9 copy-start.10
  83.9 1.2 copy-start.12
  105.0 1.4 collective-permute-start.16
  106.4 3.0 %collective-permute-start.17 = (f32[96,128]{1,0:T(8,128)S(1)}, f32[96,128]{1,0:T(8,128)S(1)}, u32[]{:S(2)}, u32[]{:S(2)}) collective-permute-start(f32[96,128]{1,0:T(8,128)S(1)} %slice_select_fusion.1), channel_id=1, source_target_pairs={{0,64},{64,0},{128,192},{192,128},{1,65},{65,1},{129,193},{193,129... | collective-permute-start | bytes 147464 | tf_op jit(solution)/shard_map/ppermute | solution.py:257
  109.4 4.3 %collective-permute-start.18 = (f32[48,128]{1,0:T(8,128)S(1)}, f32[48,128]{1,0:T(8,128)S(1)}, u32[]{:S(2)}, u32[]{:S(2)}) collective-permute-start(f32[48,128]{1,0:T(8,128)S(1)} %slice_select_fusion.2), channel_id=1, source_target_pairs={{0,128},{64,192},{128,0},{192,64},{1,129},{65,193},{129,1},{193,65... | collective-permute-start | bytes 73736 | tf_op jit(solution)/shard_map/ppermute | solution.py:257
  113.7 3.1 %collective-permute-start.19 = (f32[48,128]{1,0:T(8,128)S(1)}, f32[48,128]{1,0:T(8,128)S(1)}, u32[]{:S(2)}, u32[]{:S(2)}) collective-permute-start(f32[48,128]{1,0:T(8,128)S(1)} %select_add_fusion.2), channel_id=1, source_target_pairs={{0,16},{8,24},{16,0},{24,8},{32,48},{40,56},{48,32},{56,40},{1,17}... | collective-permute-start | bytes 73736 | tf_op jit(solution)/shard_map/ppermute | solution.py:257
  116.8 4.5 %collective-permute-start.20 = (f32[48,128]{1,0:T(8,128)S(1)}, f32[48,128]{1,0:T(8,128)S(1)}, u32[]{:S(2)}, u32[]{:S(2)}) collective-permute-start(f32[48,128]{1,0:T(8,128)S(1)} %add.47), channel_id=1, source_target_pairs={{0,32},{8,40},{16,48},{24,56},{32,0},{40,8},{48,16},{56,24},{1,33}... | collective-permute-start | bytes 73736 | tf_op jit(solution)/shard_map/ppermute | solution.py:257
  121.3 4.0 %collective-permute-start.21 = (f32[48,128]{1,0:T(8,128)S(1)}, f32[48,128]{1,0:T(8,128)S(1)}, u32[]{:S(2)}, u32[]{:S(2)}) collective-permute-start(f32[48,128]{1,0:T(8,128)S(1)} %add.48), channel_id=1, source_target_pairs={{0,1},{1,0},{2,3},{3,2},{4,5},{5,4},{6,7},{7,6},{8,9},{9,8},{10,11... | collective-permute-start | bytes 73736 | tf_op jit(solution)/shard_map/ppermute | solution.py:257
  125.3 5.7 %collective-permute-start.22 = (f32[48,128]{1,0:T(8,128)S(1)}, f32[48,128]{1,0:T(8,128)S(1)}, u32[]{:S(2)}, u32[]{:S(2)}) collective-permute-start(f32[48,128]{1,0:T(8,128)S(1)} %add.49), channel_id=1, source_target_pairs={{0,2},{1,3},{2,0},{3,1},{4,6},{5,7},{6,4},{7,5},{8,10},{9,11},{10,... | collective-permute-start | bytes 73736 | tf_op jit(solution)/shard_map/ppermute | solution.py:257
  131.1 6.6 %collective-permute-start.23 = (f32[48,128]{1,0:T(8,128)S(1)}, f32[48,128]{1,0:T(8,128)S(1)}, u32[]{:S(2)}, u32[]{:S(2)}) collective-permute-start(f32[48,128]{1,0:T(8,128)S(1)} %add.50), channel_id=1, source_target_pairs={{0,4},{1,5},{2,6},{3,7},{4,0},{5,1},{6,2},{7,3},{8,12},{9,13},{10,... | collective-permute-start | bytes 73736 | tf_op jit(solution)/shard_map/ppermute | solution.py:257
  137.7 4.2 %collective-permute-start.24 = (f32[48,128]{1,0:T(8,128)S(1)}, f32[48,128]{1,0:T(8,128)S(1)}, u32[]{:S(2)}, u32[]{:S(2)}) collective-permute-start(f32[48,128]{1,0:T(8,128)S(1)} %add.51), channel_id=1, source_target_pairs={{0,128},{64,192},{128,0},{192,64},{1,129},{65,193},{129,1},{193,65... | collective-permute-start | bytes 73736 | tf_op jit(solution)/shard_map/ppermute | solution.py:257
  141.9 3.0 %collective-permute-start.25 = (f32[96,128]{1,0:T(8,128)S(1)}, f32[96,128]{1,0:T(8,128)S(1)}, u32[]{:S(2)}, u32[]{:S(2)}) collective-permute-start(f32[96,128]{1,0:T(8,128)S(1)} %pad_maximum_fusion.11), channel_id=1, source_target_pairs={{0,64},{64,0},{128,192},{192,128},{1,65},{65,1},{129,193},{193,129... | collective-permute-start | bytes 147464 | tf_op jit(solution)/shard_map/ppermute | solution.py:257
  144.9 10.8 %collective-permute-start.26 = (f32[192,128]{1,0:T(8,128)S(1)}, f32[192,128]{1,0:T(8,128)S(1)}, u32[]{:S(2)}, u32[]{:S(2)}) collective-permute-start(f32[192,128]{1,0:T(8,128)S(1)} %pad_maximum_fusion.10), channel_id=1, source_target_pairs={{0,8},{8,0},{16,24},{24,16},{32,40},{40,32},{48,56},{56,48},{1,9},... | collective-permute-start | bytes 294920 | tf_op jit(solution)/shard_map/ppermute | solution.py:257

commit v2 on v1

v2 whole, which is shorter than its diff:
```python
import functools

import jax
import jax.numpy as jnp
import numpy as np
from jax import lax
from jax.experimental import pallas as pl
from jax.experimental.pallas import tpu as pltpu
from jax.sharding import PartitionSpec as P

F32 = jnp.float32
BF16 = jnp.bfloat16
EXACT = lax.Precision.HIGHEST
CELLS = 4
SLOTS = 10
SIDE = 256
GROUP = 4
ROOM = 48
BLOCK = 64

STAGES = (
    (
        ("own", 4), ("o", 4), ("i", 4), ("ends-", 2), ("ends+", 2),
        ("mids-", 2), ("mids+", 2), ("o2", 4), ("below2", 3), ("above2", 3),
    ),
    (("o3", 6), ("below3", 2), ("above3", 2), ("i3", 14)),
)


def place(column, dx, z):
    side = int(dx > 0)
    sign = "+" if dx > 0 else "-"
    last = int(z == CELLS - 1)
    inside = 0 <= z < CELLS
    mid = z in (1, 2)
    above = int(z > 0)
    outer = "above" if above else "below"
    if column == "own":
        if not inside:
            return (outer + "2", 0 if dx == 0 else 1 + side)
        if dx == 0:
            return ("own", z)
        return ("mids" + sign, z - 1) if mid else ("ends" + sign, last)
    if inside:
        if dx == 0:
            return (column, z)
        if mid:
            return (column + "3", 2 * side + z - 1)
        return ("o2", 2 * side + last) if column == "o" else ("i3", 10 + 2 * side + last)
    if column == "o":
        return ("o3", 4 + above) if dx == 0 else (outer + "3", side)
    return ("i3", 4 + 3 * above + (0 if dx == 0 else 1 + side))


def lookup(buffers):
    start, total = {}, 0
    for name, count in buffers:
        start[name] = total
        total += count
    table = np.full((2, CELLS, 27), -1, np.int32)
    for parity in range(2):
        for cell in range(CELLS):
            for code in range(27):
                dx, dy, dz = code // 9 - 1, code // 3 % 3 - 1, code % 3 - 1
                inner = 1 if parity == 0 else -1
                column = "own" if dy == 0 else "i" if dy == inner else "o"
                name, at = place(column, dx, cell + dz)
                if name in start:
                    table[parity, cell, code] = start[name] + at
    return table.reshape(2, CELLS * 27)


def split(values):
    high = values.astype(BF16)
    return high, (values - high.astype(F32)).astype(BF16)


def product(a, b):
    ah, al = split(a)
    bh, bl = split(b)
    return jnp.dot(
        jnp.concatenate([ah, ah, al], axis=1),
        jnp.concatenate([bh, bl, bh], axis=0),
        preferred_element_type=F32,
    )


def pack_kernel(pieces, taken, given, *refs):
    sources, outs, sem = refs[:taken], refs[given:-1], refs[-1]
    copies = []
    for out, parts in zip(outs, pieces):
        start = 0
        for source, low, count in parts:
            copy = pltpu.make_async_copy(
                sources[source].at[pl.ds(low, count)],
                out.at[pl.ds(start, count)],
                sem.at[len(copies)],
            )
            copy.start()
            copies.append(copy)
            start += count
    for copy in copies:
        copy.wait()


def pack(got, payloads, after=()):
    names = sorted({name for parts in payloads for name, _, _ in parts})
    pieces = [[(names.index(name), low, count) for name, low, count in parts] for parts in payloads]
    anywhere = pl.BlockSpec(memory_space=pl.ANY)
    return pl.pallas_call(
        functools.partial(pack_kernel, pieces, len(names), len(names) + len(after)),
        out_shape=tuple(
            jax.ShapeDtypeStruct((sum(count for _, _, count in parts), SIDE, SIDE), F32)
            for parts in payloads
        ),
        in_specs=[anywhere] * (len(names) + len(after)),
        out_specs=(anywhere,) * len(payloads),
        scratch_shapes=[pltpu.SemaphoreType.DMA((sum(map(len, payloads)),))],
        compiler_params=pltpu.CompilerParams(vmem_limit_bytes=1 << 20),
        name="pack",
    )(*(got[name] for name in names), *after)


def listed(table_ref, codes_ref, chosen, begin):
    taken = jnp.int32(0)
    for cell in range(CELLS):
        for at in range(cell * SLOTS, (cell + 1) * SLOTS):
            entry = table_ref[27 * cell + codes_ref[at]]

            @pl.when(entry >= 0)
            def _(at=at, cell=cell, entry=entry, taken=taken):
                chosen[0, taken] = jnp.int32(at)
                chosen[1, taken] = entry
                chosen[2, taken] = jnp.int32(cell)
                begin(at, taken)

            taken = taken + (entry >= 0).astype(jnp.int32)
    return taken


def multiply(taken, chosen, tile, window, arrived, total):
    for n in range(GROUP - 1):
        chosen[1, taken + n] = jnp.int32(0)
        chosen[2, taken + n] = jnp.int32(0)
        tile[taken + n] = jnp.zeros((SIDE, SIDE), F32)

    def group(g, carry):
        first = GROUP * g
        for n in range(GROUP):

            @pl.when(first + n < taken)
            def _(n=first + n):
                arrived(n)

        done = [product(tile[first + n], window[chosen[1, first + n]]) for n in range(GROUP)]
        for n in range(GROUP):
            total[chosen[2, first + n]] += done[n]
        return carry

    lax.fori_loop(0, (taken + GROUP - 1) // GROUP, group, 0)


def early_kernel(counts, table_ref, later_ref, codes_ref, tiles_ref, *rest):
    buffers, rest = rest[: len(counts)], rest[len(counts) :]
    out_ref, list_ref, window, tile, chosen, window_sem, tile_sem = rest
    copies, start = [], 0
    for n, (count, ref) in enumerate(zip(counts, buffers)):
        copy = pltpu.make_async_copy(ref, window.at[pl.ds(start, count)], window_sem.at[n])
        copy.start()
        copies.append(copy)
        start += count

    def fetch(at, n):
        return pltpu.make_async_copy(tiles_ref.at[at], tile.at[n], tile_sem.at[n])

    taken = listed(table_ref, codes_ref, chosen, lambda at, n: fetch(at, n).start())
    list_ref[0, ROOM - 1] = listed(later_ref, codes_ref, list_ref, lambda at, n: None)
    for copy in copies:
        copy.wait()
    for cell in range(CELLS):
        out_ref[cell] = -0.5 * window[cell]
    multiply(taken, chosen, tile, window, lambda n: fetch(0, n).wait(), out_ref)


def late_kernel(counts, list_ref, tiles_ref, before_ref, *rest):
    buffers, rest = rest[: len(counts)], rest[len(counts) :]
    out_ref, gram_ref, total, window, tile, chosen, window_sem, tile_sem, sems = rest
    taken = list_ref[0, ROOM - 1]

    def fetch(at, n):
        return pltpu.make_async_copy(tiles_ref.at[at], tile.at[n], tile_sem.at[n])

    def begin(n, carry):
        entry = list_ref[1, n]
        chosen[1, n] = n
        chosen[2, n] = list_ref[2, n]
        fetch(list_ref[0, n], n).start()
        start = 0
        for count, ref in zip(counts, buffers):

            @pl.when((entry >= start) & (entry < start + count))
            def _(ref=ref, start=start):
                pltpu.make_async_copy(ref.at[entry - start], window.at[n], window_sem.at[n]).start()

            start += count
        return carry

    def arrived(n):
        fetch(0, n).wait()
        pltpu.make_async_copy(buffers[0].at[0], window.at[n], window_sem.at[n]).wait()

    lax.fori_loop(0, taken, begin, 0)
    before = pltpu.make_async_copy(before_ref, total, sems.at[CELLS])
    before.start()
    before.wait()
    multiply(taken, chosen, tile, window, arrived, total)
    copies = [
        pltpu.make_async_copy(total.at[cell], out_ref.at[cell], sems.at[cell]) for cell in range(CELLS)
    ]
    for copy in copies:
        copy.start()
    gram = jnp.zeros((SIDE, SIDE), F32)
    for cell in range(CELLS):
        high, low = split(total[cell])
        gram += lax.dot_general(
            jnp.concatenate([high, high, low], axis=0),
            jnp.concatenate([high, low, high], axis=0),
            (((0,), (0,)), ((), ())),
            preferred_element_type=F32,
        )
    gram_ref[...] = gram
    for copy in copies:
        copy.wait()


SMEM = pl.BlockSpec(memory_space=pltpu.SMEM)
FAR = pl.BlockSpec(memory_space=pltpu.HBM)
NEAR = pl.BlockSpec(memory_space=pltpu.VMEM)
SLOT_ROOM = CELLS * SLOTS + GROUP


def apply(odd, codes, tiles, got):
    early, late = STAGES
    tables = [jnp.where(odd, jnp.asarray(t[1]), jnp.asarray(t[0])) for t in map(lookup, STAGES)]
    counts = tuple(count for _, count in early)
    panel = jax.ShapeDtypeStruct((CELLS, SIDE, SIDE), F32)
    chosen = pltpu.SMEM((3, SLOT_ROOM), jnp.int32)
    tile = pltpu.VMEM((SLOT_ROOM, SIDE, SIDE), F32)
    params = pltpu.CompilerParams(vmem_limit_bytes=60 << 20)
    cost = pl.CostEstimate(
        flops=SLOTS * CELLS * 2 * SIDE**3, bytes_accessed=12 << 20, transcendentals=0
    )
    part, left = pl.pallas_call(
        functools.partial(early_kernel, counts),
        out_shape=(panel, jax.ShapeDtypeStruct((3, ROOM), jnp.int32)),
        in_specs=[SMEM, SMEM, SMEM, FAR] + [FAR] * len(counts),
        out_specs=(NEAR, SMEM),
        scratch_shapes=[
            pltpu.VMEM((sum(counts), SIDE, SIDE), F32),
            tile,
            chosen,
            pltpu.SemaphoreType.DMA((len(counts),)),
            pltpu.SemaphoreType.DMA((SLOT_ROOM,)),
        ],
        compiler_params=params,
        cost_estimate=cost,
        name="apply_early",
    )(*tables, codes, tiles, *(got[name] for name, _ in early))
    counts = tuple(count for _, count in late)
    return pl.pallas_call(
        functools.partial(late_kernel, counts),
        out_shape=(panel, jax.ShapeDtypeStruct((SIDE, SIDE), F32)),
        in_specs=[SMEM, FAR, FAR] + [FAR] * len(counts),
        out_specs=(FAR, NEAR),
        scratch_shapes=[
            pltpu.VMEM((CELLS, SIDE, SIDE), F32),
            tile,
            tile,
            chosen,
            pltpu.SemaphoreType.DMA((SLOT_ROOM,)),
            pltpu.SemaphoreType.DMA((SLOT_ROOM,)),
            pltpu.SemaphoreType.DMA((CELLS + 1,)),
        ],
        compiler_params=params,
        cost_estimate=cost,
        name="apply_late",
    )(left, tiles, part, *(got[name] for name, _ in late))


def leaf(rows):
    rows = list(rows)
    at = lax.broadcasted_iota(jnp.int32, (8, 128), 0)
    count = len(rows)
    for b in range(count):
        rest = range(b, count)
        column = {
            (k, v): jnp.broadcast_to(rows[v][:, 8 * b + k : 8 * b + k + 1], (8, 128))
            for k in range(8)
            for v in rest
        }
        for j in range(8):
            scale = lax.rsqrt(jnp.broadcast_to(column[j, b][j : j + 1], (8, 128)))
            times = {v: column[j, v] * scale for v in rest}
            times[b] = jnp.where(at > j, times[b], 0.0)
            for k in range(j + 1, 8):
                pivot = jnp.broadcast_to(column[k, b][j : j + 1], (8, 128)) * scale
                for v in rest:
                    column[k, v] = column[k, v] - times[v] * pivot
            pivot = jnp.broadcast_to(rows[b][j : j + 1], (8, 128)) * scale
            for v in rest:
                if v > b:
                    rows[v] = rows[v] - times[v] * pivot
            rows[b] = jnp.where(at == j, pivot, rows[b] - times[b] * pivot)
    return rows


def factor_kernel(total, gram_ref, filtered_ref, bands_ref, factor_ref, work, filtered, bands, sems):
    fetch = pltpu.make_async_copy(filtered_ref, filtered, sems.at[CELLS])
    fetch.start()
    row = lax.broadcasted_iota(jnp.int32, (SIDE, SIDE), 0)
    col = lax.broadcasted_iota(jnp.int32, (SIDE, SIDE), 1)
    work[:, :SIDE] = gram_ref[...] * (1.0 / total)
    work[:, SIDE:] = (row == col).astype(F32)
    eye = (row == col)[:BLOCK, :BLOCK].astype(F32)
    for low in range(0, SIDE, BLOCK):
        high = low + BLOCK
        rows = pl.ds(low, BLOCK)
        block = jnp.concatenate([work[rows, low:high], eye], axis=1)
        done = jnp.concatenate(leaf([block[8 * v : 8 * v + 8] for v in range(BLOCK // 8)]), axis=0)
        solved = jnp.dot(done[:, BLOCK:], work[rows, :], precision=EXACT, preferred_element_type=F32)
        work[rows, :] = solved
        if high < SIDE:
            under = pl.ds(high, SIDE - high)
            work[under, :] = work[under, :] - lax.dot_general(
                solved[:, high:SIDE],
                solved,
                (((0,), (0,)), ((), ())),
                precision=EXACT,
                preferred_element_type=F32,
            )
    factor_ref[...] = jnp.where(row <= col, work[:, :SIDE], 0.0)
    high, low = split(jnp.where(row >= col, work[:, SIDE:], 0.0))
    right = jnp.concatenate([high, low, high], axis=1)
    fetch.wait()
    copies = []
    for cell in range(CELLS):
        fh, fl = split(filtered[cell])
        bands[cell] = lax.dot_general(
            jnp.concatenate([fh, fh, fl], axis=1),
            right,
            (((1,), (1,)), ((), ())),
            preferred_element_type=F32,
        )
        copies.append(pltpu.make_async_copy(bands.at[cell], bands_ref.at[cell], sems.at[cell]))
        copies[cell].start()
    for copy in copies:
        copy.wait()


def factorise(gram, filtered, total):
    vmem = pl.BlockSpec(memory_space=pltpu.VMEM)
    far = pl.BlockSpec(memory_space=pltpu.HBM)
    panel = (CELLS, SIDE, SIDE)
    return pl.pallas_call(
        functools.partial(factor_kernel, total),
        out_shape=(jax.ShapeDtypeStruct(panel, F32), jax.ShapeDtypeStruct((SIDE, SIDE), F32)),
        in_specs=[vmem, far],
        out_specs=(far, vmem),
        scratch_shapes=[
            pltpu.VMEM((SIDE, 2 * SIDE), F32),
            pltpu.VMEM(panel, F32),
            pltpu.VMEM(panel, F32),
            pltpu.SemaphoreType.DMA((CELLS + 1,)),
        ],
        compiler_params=pltpu.CompilerParams(vmem_limit_bytes=62_488_000),
        name="factorise",
    )(gram, filtered)


def flip(values, axis, bit):
    size = lax.axis_size(axis)
    return lax.ppermute(values, axis, [(i, i ^ bit) for i in range(size)])


def exchange(pieces, axes):
    return lax.all_to_all(pieces, axes, 0, 0).reshape(pieces.shape)


def summed(gram):
    plane = ("gx", "gy")
    peers, planes = lax.axis_size("gx") * lax.axis_size("gy"), lax.axis_size("gz")
    rows = exchange(gram.reshape(peers, SIDE // peers, SIDE), plane).sum(0)
    rows = exchange(jnp.broadcast_to(rows, (planes, *rows.shape)), "gz").sum(0)
    return exchange(jnp.broadcast_to(rows, (peers, *rows.shape)), plane).reshape(SIDE, SIDE)


def up(values, axis):
    return lax.ppermute(values, axis, [(i, i + 1) for i in range(lax.axis_size(axis) - 1)])


def down(values, axis):
    return lax.ppermute(values, axis, [(i + 1, i) for i in range(lax.axis_size(axis) - 1)])


def across(values):
    size = lax.axis_size("gy")
    pairs = [(i, i + 1) for i in range(1, size - 1, 2)]
    return lax.ppermute(values, "gy", pairs + [(j, i) for i, j in pairs])


def per_device(panel, tiles, codes):
    top = CELLS - 1
    own = panel[0, 0]
    odd = lax.axis_index("gy") % 2 == 1
    tiles = tiles.reshape(CELLS * SLOTS, SIDE, SIDE)
    codes = codes.reshape(CELLS * SLOTS)

    ends = jnp.concatenate([own[:1], own[top:]], axis=0)
    got = {"own": own}
    got["ends-"], got["ends+"] = up(ends, "gx"), down(ends, "gx")
    got["o"] = across(own)
    got["i"] = flip(own, "gy", 1)

    sides, tops, bottoms, mids = pack(
        got,
        [
            [("ends-", 0, 2), ("ends+", 0, 2)],
            [("own", top, 1), ("ends-", 1, 1), ("ends+", 1, 1)],
            [("own", 0, 1), ("ends-", 0, 1), ("ends+", 0, 1)],
            [("own", 1, 2)],
        ],
        after=(got["o"], got["i"]),
    )
    got["o2"] = across(sides)
    got["below2"], got["above2"] = up(tops, "gz"), down(bottoms, "gz")
    got["mids-"], got["mids+"] = up(mids, "gx"), down(mids, "gx")

    outer, tops, bottoms, inner = pack(
        got,
        [
            [("mids-", 0, 2), ("mids+", 0, 2), ("below2", 0, 1), ("above2", 0, 1)],
            [("o2", 1, 1), ("o2", 3, 1)],
            [("o2", 0, 1), ("o2", 2, 1)],
            [
                ("mids-", 0, 2), ("mids+", 0, 2), ("below2", 0, 3), ("above2", 0, 3),
                ("ends-", 0, 2), ("ends+", 0, 2),
            ],
        ],
    )
    got["o3"] = across(outer)
    got["below3"], got["above3"] = up(tops, "gz"), down(bottoms, "gz")
    got["i3"] = flip(inner, "gy", 1)

    filtered, gram = apply(odd, codes, tiles, got)
    devices = lax.axis_size("gx") * lax.axis_size("gy") * lax.axis_size("gz")
    bands, factor = factorise(summed(gram), filtered, CELLS * SIDE * devices)
    return bands.reshape(panel.shape), factor


def solution(mesh):
    in_specs = (
        P("gx", "gy", "gz", None, None),
        P("gx", "gy", "gz", None, None, None),
        P("gx", "gy", "gz", None),
    )
    out_specs = (P("gx", "gy", "gz", None, None), P())
    return jax.shard_map(
        per_device, mesh=mesh, in_specs=in_specs, out_specs=out_specs, check_vma=False
    )
```

time: 168 us -> 151 us (0.90)
  blocking collectives: 0 us -> 47.5 us
  starting transfers between devices: 72 us -> 37.1 us
  waiting for transfers between devices: 46.8 us -> 21.8 us
  Pallas kernels: 30.9 us -> 37.4 us
  other arithmetic: 5.92 us -> 0.69 us
  local copies, waits for them, and re-layouts: 10.2 us -> 5.09 us
    all_to_all x0 -> x3, blocking collectives: none -> 47.5 us  [exchange(): return lax.all_to_all(pieces, axes, 0, 0).reshape(pieces.shape)]
    ppermute x14 -> x2, starting transfers between devices: 33.5 us -> 3.35 us  [flip(): return lax.ppermute(values, axis, [(i, i ^ bit) for i in range(size)])]
    ppermute x14 -> x2, waiting for transfers between devices: 18 us -> 0.01 us  [flip(): return lax.ppermute(values, axis, [(i, i ^ bit) for i in range(size)])]
    ppermute x5 -> x4, waiting for transfers between devices: 15.7 us -> 3.51 us  [up(): lax.ppermute(values, axis, [(i, i + 1) for i in range(lax.axis_size(axis)...]
    ppermute x5 -> x4, waiting for transfers between devices: 6.51 us -> 17.1 us  [down(): lax.ppermute(values, axis, [(i + 1, i) for i in range(lax.axis_size(axis)...]
    concatenate x12 -> x1, other arithmetic: 5.79 us -> 0.04 us  [per_device(): ends = jnp.concatenate([own[:1], own[top:]], axis=0)]
    ppermute x3, waiting for transfers between devices: 6.59 us -> 1.12 us  [across(): return lax.ppermute(values, 'gy', pairs + [(j, i) for i, j in pairs])]
    unnamed x36, local copies, waits for them, and re-layouts: 8.73 us -> 3.34 us
  transfers between devices with their start and end apart: 27 -> 13, of which waited for: 16 -> 6; matrix products, arithmetic and copies ran while one was open for 4% -> 2% of each run, Pallas kernels for 7% -> 7%
where the time goes in v2:
time: 151 us
  blocking collectives  47.5 us (31%)
  Pallas kernels  37.4 us (25%)
  starting transfers between devices  37.1 us (25%)
  waiting for transfers between devices  21.8 us (14%)
  local copies, waits for them, and re-layouts  5.09 us (3%)
    all_to_all x3, blocking collectives, exchange(): return lax.all_to_all(pieces, axes, 0, 0).reshape(pieces.shape)  47.5 us
    ppermute x4, waiting for transfers between devices, down(): lax.ppermute(values, axis, [(i + 1, i) for i in range(lax.axis_size(axis)...  17.1 us
    ppermute x4, starting transfers between devices, up(): lax.ppermute(values, axis, [(i, i + 1) for i in range(lax.axis_size(axis)...  15.9 us
    pallas_call x1, Pallas kernels, factorise(): pl.pallas_call(functools.partial(factor_kernel, total), out_shape=(jax.Sh...  13.7 us
    ppermute x3, starting transfers between devices, across(): return lax.ppermute(values, 'gy', pairs + [(j, i) for i, j in pairs])  12.7 us
    pallas_call x1, Pallas kernels, apply(): pl.pallas_call(functools.partial(early_kernel, counts), out_shape=(panel,...  11 us
    pallas_call x1, Pallas kernels, apply(): pl.pallas_call(functools.partial(late_kernel, counts), out_shape=(panel,...  9.51 us
    ppermute x4, starting transfers between devices, down(): lax.ppermute(values, axis, [(i + 1, i) for i in range(lax.axis_size(axis)...  5.17 us
  transfers between devices with their start and end apart: 13, of which 6 were waited for; matrix products, arithmetic and copies ran while one was open for 2% of the time, Pallas kernels for 7%

profile of v2, /device:TPU:1, one launch (start us, length us, event | category | flops | bytes accessed | tf_op | source)
XLA Modules:
  0.0 150.7 jit_solution(17260456118675254350)
XLA Ops:
  0.6 3.3 %collective-permute-start.1 = (f32[4,256,256]{2,1,0:T(8,128)}, f32[4,256,256]{2,1,0:T(8,128)S(1)}, u32[]{:S(2)}, u32[]{:S(2)}) collective-permute-start(f32[4,256,256]{2,1,0:T(8,128)} %bitcast.9), channel_id=1, source_target_pairs={{0,8},{8,0},{16,24},{24,16},{32,40},{40,32},{48,56},{56,48},{1,9},... | collective-permute-start | bytes 3145736 | tf_op jit(solution)/shard_map/ppermute | solution.py:382
  4.0 1.9 %collective-permute-start = (f32[4,256,256]{2,1,0:T(8,128)}, f32[4,256,256]{2,1,0:T(8,128)S(1)}, u32[]{:S(2)}, u32[]{:S(2)}) collective-permute-start(f32[4,256,256]{2,1,0:T(8,128)} %bitcast.10), channel_id=1, source_target_pairs={{8,16},{24,32},{40,48},{16,8},{32,24},{48,40},{9,17},{25,33},{41,4... | collective-permute-start | bytes 3145736 | tf_op jit(solution)/shard_map/ppermute | solution.py:408
  5.9 1.1 slice_bitcast_fusion.1
  6.9 0.0 copy-start.13
  7.0 0.0 copy-start.14
  7.0 0.0 copy-start.15
  7.0 0.0 copy-start.16
  7.0 0.0 copy-start.17
  7.1 1.3 collective-permute-start.3
  8.4 4.0 %collective-permute-start.2 = (f32[2,256,256]{2,1,0:T(8,128)S(1)}, f32[2,256,256]{2,1,0:T(8,128)S(1)}, u32[]{:S(2)}, u32[]{:S(2)}) collective-permute-start(f32[2,256,256]{2,1,0:T(8,128)S(1)} %pad_maximum_fusion), channel_id=1, source_target_pairs={{0,64},{64,128},{128,192},{1,65},{65,129},{129,193},{2,66},{66,130... | collective-permute-start | bytes 1572872 | tf_op jit(solution)/shard_map/ppermute | solution.py:398
  12.4 9.5 %collective-permute-done.3.refs_0_.rest_4_.refs_2_ = f32[2,256,256]{2,1,0:T(8,128)S(1)} collective-permute-done((f32[2,256,256]{2,1,0:T(8,128)S(1)}, f32[2,256,256]{2,1,0:T(8,128)S(1)}, u32[]{:S(2)}, u32[]{:S(2)}) %collective-permute-start.3) | collective-permute-done | bytes 524320 | tf_op jit(solution)/shard_map/ppermute | solution.py:402
  21.9 0.0 copy-start.1
  21.9 1.8 %collective-permute-done.2.refs_1_.rest_3_.refs_3_ = f32[2,256,256]{2,1,0:T(8,128)S(1)} collective-permute-done((f32[2,256,256]{2,1,0:T(8,128)S(1)}, f32[2,256,256]{2,1,0:T(8,128)S(1)}, u32[]{:S(2)}, u32[]{:S(2)}) %collective-permute-start.2) | collective-permute-done | bytes 524320 | tf_op jit(solution)/shard_map/ppermute | solution.py:398
  23.6 0.0 collective-permute-done.1.refs_4_.rest_2_
  23.7 0.0 collective-permute-done.refs_3_.rest_1_
  23.7 0.0 copy-start
  23.7 1.8 %copy-done = f32[1,1,4,256,256]{4,3,2,1,0:T(8,128)S(1)} copy-done((f32[1,1,4,256,256]{4,3,2,1,0:T(8,128)S(1)}, f32[1,1,4,256,256]{4,3,2,1,0:T(8,128)}, u32[]{:S(2)}) %copy-start) | copy-done | bytes 1048600
  25.5 0.3 pack.2
  25.8 3.4 %collective-permute-start.6 = (f32[4,256,256]{2,1,0:T(8,128)S(1)}, f32[4,256,256]{2,1,0:T(8,128)S(1)}, u32[]{:S(2)}, u32[]{:S(2)}) collective-permute-start(f32[4,256,256]{2,1,0:T(8,128)S(1)} %get-tuple-element.17), channel_id=1, source_target_pairs={{8,16},{24,32},{40,48},{16,8},{32,24},{48,40},{9,17},{25,33},{41,4... | collective-permute-start | bytes 3145736 | tf_op jit(solution)/shard_map/ppermute | solution.py:408
  29.2 3.6 %collective-permute-start.7 = (f32[3,256,256]{2,1,0:T(8,128)S(1)}, f32[3,256,256]{2,1,0:T(8,128)S(1)}, u32[]{:S(2)}, u32[]{:S(2)}) collective-permute-start(f32[3,256,256]{2,1,0:T(8,128)S(1)} %get-tuple-element.18), channel_id=1, source_target_pairs={{0,1},{1,2},{2,3},{3,4},{4,5},{5,6},{6,7},{8,9},{9,10},{10,11},{11... | collective-permute-start | bytes 2359304 | tf_op jit(solution)/shard_map/ppermute | solution.py:398
  32.8 1.3 collective-permute-start.8
  34.0 1.3 collective-permute-start.5
  35.4 4.8 %collective-permute-start.4 = (f32[2,256,256]{2,1,0:T(8,128)S(1)}, f32[2,256,256]{2,1,0:T(8,128)S(1)}, u32[]{:S(2)}, u32[]{:S(2)}) collective-permute-start(f32[2,256,256]{2,1,0:T(8,128)S(1)} %get-tuple-element.16), channel_id=1, source_target_pairs={{0,64},{64,128},{128,192},{1,65},{65,129},{129,193},{2,66},{66,130... | collective-permute-start | bytes 1572872 | tf_op jit(solution)/shard_map/ppermute | solution.py:398
  40.1 5.5 %collective-permute-done.5.rest_6_.refs_4_ = f32[2,256,256]{2,1,0:T(8,128)S(1)} collective-permute-done((f32[2,256,256]{2,1,0:T(8,128)S(1)}, f32[2,256,256]{2,1,0:T(8,128)S(1)}, u32[]{:S(2)}, u32[]{:S(2)}) %collective-permute-start.5) | collective-permute-done | bytes 524320 | tf_op jit(solution)/shard_map/ppermute | solution.py:402
  45.7 1.8 %collective-permute-done.4.rest_5_.refs_5_ = f32[2,256,256]{2,1,0:T(8,128)S(1)} collective-permute-done((f32[2,256,256]{2,1,0:T(8,128)S(1)}, f32[2,256,256]{2,1,0:T(8,128)S(1)}, u32[]{:S(2)}, u32[]{:S(2)}) %collective-permute-start.4) | collective-permute-done | bytes 524320 | tf_op jit(solution)/shard_map/ppermute | solution.py:398
  47.4 0.0 collective-permute-done.7.rest_8_.refs_1_
  47.4 2.1 %collective-permute-done.8.rest_9_.refs_0_ = f32[3,256,256]{2,1,0:T(8,128)S(1)} collective-permute-done((f32[3,256,256]{2,1,0:T(8,128)S(1)}, f32[3,256,256]{2,1,0:T(8,128)S(1)}, u32[]{:S(2)}, u32[]{:S(2)}) %collective-permute-start.8) | collective-permute-done | bytes 786464 | tf_op jit(solution)/shard_map/ppermute | solution.py:402
  49.5 0.0 collective-permute-done.6.rest_7_.refs_6_
  49.5 2.8 %pack.3 = (f32[6,256,256]{2,1,0:T(8,128)}, f32[2,256,256]{2,1,0:T(8,128)}, f32[2,256,256]{2,1,0:T(8,128)}, f32[14,256,256]{2,1,0:T(8,128)}) custom-call(f32[3,256,256]{2,1,0:T(8,128)S(1)} %collective-permute-done.8.rest_9_.refs_0_, f32[3,256,256]{2,1,0:T(8,128)S(1)} %collective-permute-done.7.rest_8_.refs_1_, ...), custom_call_target="tpu_custom_call" | custom-call | tf_op jit(solution)/shard_map/pack/pallas_call | solution.py:110
  52.3 0.0 copy-done.1
  52.4 0.0 copy-done.2
  52.4 0.0 copy-done.3
  52.4 0.0 copy-done.4
  52.4 0.1 copy-done.5
  52.5 0.0 collective-permute-start.12
  52.5 0.0 copy-done.6
  52.5 0.2 copy-done.7
  52.7 7.5 %collective-permute-start.9 = (f32[6,256,256]{2,1,0:T(8,128)}, f32[6,256,256]{2,1,0:T(8,128)S(1)}, u32[]{:S(2)}, u32[]{:S(2)}) collective-permute-start(f32[6,256,256]{2,1,0:T(8,128)} %get-tuple-element.22), channel_id=1, source_target_pairs={{8,16},{24,32},{40,48},{16,8},{32,24},{48,40},{9,17},{25,33},{41,4... | collective-permute-start | bytes 4718600 | tf_op jit(solution)/shard_map/ppermute | solution.py:408
  60.2 0.0 copy-done.8
  60.2 0.0 copy-done.9
  60.2 3.5 %collective-permute-start.10 = (f32[2,256,256]{2,1,0:T(8,128)}, f32[2,256,256]{2,1,0:T(8,128)S(1)}, u32[]{:S(2)}, u32[]{:S(2)}) collective-permute-start(f32[2,256,256]{2,1,0:T(8,128)} %get-tuple-element.23), channel_id=1, source_target_pairs={{0,1},{1,2},{2,3},{3,4},{4,5},{5,6},{6,7},{8,9},{9,10},{10,11},{11... | collective-permute-start | bytes 1572872 | tf_op jit(solution)/shard_map/ppermute | solution.py:398
  63.7 1.3 collective-permute-start.11
  65.0 0.0 copy-done.13
  65.0 0.7 reshape.21.codes_ref
  65.7 0.0 copy-done.14
  65.7 0.0 copy-done.15
  65.7 0.0 copy-done.16
  65.7 0.0 copy-done.17
  65.7 0.6 broadcast_select_fusion
  66.3 11.0 %apply_early.1 = (f32[4,256,256]{2,1,0:T(8,128)}, s32[3,48]{1,0:T(4,128)}) custom-call(s32[108]{0:T(128)} %get-tuple-element.33.table_ref, s32[108]{0:T(128)} %get-tuple-element.32.later_ref, s32[40]{0:T(128)} %reshape.21.codes_ref, f32[40,256,256]{2,1,0:T(8,128)} %bitcast.13, f32[4,256,256]{2,1,0:T(8,128)} %bitcast.11, f32[4,256,256]{2,1,0:T(8,128)} %copy-done.4, ...), custom_call_target="tpu_custom_call" | custom-call | flops 1342177280 | bytes 12582912 | tf_op jit(solution)/shard_map/apply_early/pallas_call | solution.py:253
  77.3 0.0 collective-permute-done.10.rest_1_
  77.3 0.0 copy-start.11
  77.3 0.0 collective-permute-done.11.rest_2_
  77.3 0.0 copy-start.12
  77.3 1.1 collective-permute-done.9.rest_0_
  78.5 0.0 collective-permute-done.12.rest_3_
  78.5 0.0 copy-done.11
  78.5 0.0 copy-done.12
  78.5 1.2 copy-done.10
  79.7 9.5 %apply_late.1 = (f32[4,256,256]{2,1,0:T(8,128)}, f32[256,256]{1,0:T(8,128)}) custom-call(s32[3,48]{1,0:T(4,128)} %get-tuple-element.20.list_ref, f32[40,256,256]{2,1,0:T(8,128)} %bitcast.14, f32[4,256,256]{2,1,0:T(8,128)} %get-tuple-element.21.before_ref, f32[6,256,256]{2,1,0:T(8,128)} %copy-done.10, f32[2,256,256]{2,1,0:T(8,128)} %copy-done.11, ...), custom_call_target="tpu_custom_call" | custom-call | flops 1342177280 | bytes 12582912 | tf_op jit(solution)/shard_map/apply_late/pallas_call | solution.py:270
  89.2 19.1 %all_to_all.15 = f32[32,8,256]{2,1,0:T(8,128)S(1)} all-to-all(f32[32,8,256]{2,1,0:T(8,128)} %bitcast.16), channel_id=1, replica_groups=mesh['gx'=4,'gy'=8,'gz'=8] {'gx','gy'}, dimensions={0} | all-to-all | bytes 524288 | tf_op jit(solution)/shard_map/all_to_all | solution.py:386
  108.4 14.3 %all_to_all.16 = f32[8,8,256]{2,1,0:T(8,128)S(1)} all-to-all(f32[8,8,256]{2,1,0:T(8,128)S(1)} %broadcast_in_dim.6), channel_id=1, replica_groups=mesh['gx'=4,'gy'=8,'gz'=8] {'gz'}, dimensions={0} | all-to-all | bytes 131072 | tf_op jit(solution)/shard_map/all_to_all | solution.py:386
  122.7 14.1 %all_to_all.17 = f32[32,8,256]{2,1,0:T(8,128)} all-to-all(f32[32,8,256]{2,1,0:T(8,128)S(1)} %broadcast_in_dim.7), channel_id=1, replica_groups=mesh['gx'=4,'gy'=8,'gz'=8] {'gx','gy'}, dimensions={0} | all-to-all | bytes 524288 | tf_op jit(solution)/shard_map/all_to_all | solution.py:386
  136.8 13.7 %factorise.1 = (f32[4,256,256]{2,1,0:T(8,128)}, f32[256,256]{1,0:T(8,128)}) custom-call(f32[256,256]{1,0:T(8,128)} %bitcast.15, f32[4,256,256]{2,1,0:T(8,128)} %get-tuple-element.27.filtered_ref), custom_call_target="tpu_custom_call" | custom-call | tf_op jit(solution)/shard_map/factorise/pallas_call | solution.py:364
  (14 shorter events, 0.1 us)
Async XLA Ops:
  0.6 23.0 %collective-permute-start.1 = (f32[4,256,256]{2,1,0:T(8,128)}, f32[4,256,256]{2,1,0:T(8,128)S(1)}, u32[]{:S(2)}, u32[]{:S(2)}) collective-permute-start(f32[4,256,256]{2,1,0:T(8,128)} %bitcast.9), channel_id=1, source_target_pairs={{0,8},{8,0},{16,24},{24,16},{32,40},{40,32},{48,56},{56,48},{1,9},... | collective-permute-start | bytes 3145736 | tf_op jit(solution)/shard_map/ppermute | solution.py:382
  4.0 19.7 %collective-permute-start = (f32[4,256,256]{2,1,0:T(8,128)}, f32[4,256,256]{2,1,0:T(8,128)S(1)}, u32[]{:S(2)}, u32[]{:S(2)}) collective-permute-start(f32[4,256,256]{2,1,0:T(8,128)} %bitcast.10), channel_id=1, source_target_pairs={{8,16},{24,32},{40,48},{16,8},{32,24},{48,40},{9,17},{25,33},{41,4... | collective-permute-start | bytes 3145736 | tf_op jit(solution)/shard_map/ppermute | solution.py:408
  6.9 58.0 %copy-start.13 = (s32[1,1,4,10]{3,2,1,0:T(4,128)S(1)}, s32[1,1,4,10]{3,2,1,0:T(4,128)}, u32[]{:S(2)}) copy-start(s32[1,1,4,10]{3,2,1,0:T(4,128)} %param.9) | copy-start | bytes 484
  7.0 58.7 %copy-start.14 = (s32[108]{0:T(128)S(1)}, s32[108]{0:T(128)}, u32[]{:S(2)}) copy-start(s32[108]{0:T(128)} %constant.32.clone) | copy-start | bytes 1300
  7.0 58.7 %copy-start.15 = (s32[108]{0:T(128)S(1)}, s32[108]{0:T(128)}, u32[]{:S(2)}) copy-start(s32[108]{0:T(128)} %constant.31.clone) | copy-start | bytes 1300
  7.0 58.7 %copy-start.16 = (s32[108]{0:T(128)S(1)}, s32[108]{0:T(128)}, u32[]{:S(2)}) copy-start(s32[108]{0:T(128)} %constant.30.clone) | copy-start | bytes 1300
  7.0 58.7 %copy-start.17 = (s32[108]{0:T(128)S(1)}, s32[108]{0:T(128)}, u32[]{:S(2)}) copy-start(s32[108]{0:T(128)} %constant.29.clone) | copy-start | bytes 1300
  7.1 14.8 %collective-permute-start.3 = (f32[2,256,256]{2,1,0:T(8,128)S(1)}, f32[2,256,256]{2,1,0:T(8,128)S(1)}, u32[]{:S(2)}, u32[]{:S(2)}) collective-permute-start(f32[2,256,256]{2,1,0:T(8,128)S(1)} %pad_maximum_fusion), channel_id=1, source_target_pairs={{64,0},{128,64},{192,128},{65,1},{129,65},{193,129},{66,2},{130,66... | collective-permute-start | bytes 1572872 | tf_op jit(solution)/shard_map/ppermute | solution.py:402
  8.4 15.3 %collective-permute-start.2 = (f32[2,256,256]{2,1,0:T(8,128)S(1)}, f32[2,256,256]{2,1,0:T(8,128)S(1)}, u32[]{:S(2)}, u32[]{:S(2)}) collective-permute-start(f32[2,256,256]{2,1,0:T(8,128)S(1)} %pad_maximum_fusion), channel_id=1, source_target_pairs={{0,64},{64,128},{128,192},{1,65},{65,129},{129,193},{2,66},{66,130... | collective-permute-start | bytes 1572872 | tf_op jit(solution)/shard_map/ppermute | solution.py:398
  21.9 30.5 %copy-start.1 = (f32[2,256,256]{2,1,0:T(8,128)}, f32[2,256,256]{2,1,0:T(8,128)S(1)}, u32[]{:S(2)}) copy-start(f32[2,256,256]{2,1,0:T(8,128)S(1)} %collective-permute-done.3.refs_0_.rest_4_.refs_2_) | copy-start | bytes 1572868
  23.6 28.7 %copy-start.2 = (f32[2,256,256]{2,1,0:T(8,128)}, f32[2,256,256]{2,1,0:T(8,128)S(1)}, u32[]{:S(2)}) copy-start(f32[2,256,256]{2,1,0:T(8,128)S(1)} %collective-permute-done.2.refs_1_.rest_3_.refs_3_) | copy-start | bytes 1572868
  23.6 28.7 %copy-start.3 = (f32[4,256,256]{2,1,0:T(8,128)}, f32[4,256,256]{2,1,0:T(8,128)S(1)}, u32[]{:S(2)}) copy-start(f32[4,256,256]{2,1,0:T(8,128)S(1)} %collective-permute-done.1.refs_4_.rest_2_) | copy-start | bytes 3145732
  23.7 1.8 %copy-start = (f32[1,1,4,256,256]{4,3,2,1,0:T(8,128)S(1)}, f32[1,1,4,256,256]{4,3,2,1,0:T(8,128)}, u32[]{:S(2)}) copy-start(f32[1,1,4,256,256]{4,3,2,1,0:T(8,128)} %param.7) | copy-start | bytes 3145732
  25.5 26.9 %copy-start.4 = (f32[4,256,256]{2,1,0:T(8,128)}, f32[4,256,256]{2,1,0:T(8,128)S(1)}, u32[]{:S(2)}) copy-start(f32[4,256,256]{2,1,0:T(8,128)S(1)} %collective-permute-done.refs_3_.rest_1_) | copy-start | bytes 3145732
  25.8 23.8 %collective-permute-start.6 = (f32[4,256,256]{2,1,0:T(8,128)S(1)}, f32[4,256,256]{2,1,0:T(8,128)S(1)}, u32[]{:S(2)}, u32[]{:S(2)}) collective-permute-start(f32[4,256,256]{2,1,0:T(8,128)S(1)} %get-tuple-element.17), channel_id=1, source_target_pairs={{8,16},{24,32},{40,48},{16,8},{32,24},{48,40},{9,17},{25,33},{41,4... | collective-permute-start | bytes 3145736 | tf_op jit(solution)/shard_map/ppermute | solution.py:408
  29.2 18.3 %collective-permute-start.7 = (f32[3,256,256]{2,1,0:T(8,128)S(1)}, f32[3,256,256]{2,1,0:T(8,128)S(1)}, u32[]{:S(2)}, u32[]{:S(2)}) collective-permute-start(f32[3,256,256]{2,1,0:T(8,128)S(1)} %get-tuple-element.18), channel_id=1, source_target_pairs={{0,1},{1,2},{2,3},{3,4},{4,5},{5,6},{6,7},{8,9},{9,10},{10,11},{11... | collective-permute-start | bytes 2359304 | tf_op jit(solution)/shard_map/ppermute | solution.py:398
  32.8 16.8 %collective-permute-start.8 = (f32[3,256,256]{2,1,0:T(8,128)S(1)}, f32[3,256,256]{2,1,0:T(8,128)S(1)}, u32[]{:S(2)}, u32[]{:S(2)}) collective-permute-start(f32[3,256,256]{2,1,0:T(8,128)S(1)} %get-tuple-element.19), channel_id=1, source_target_pairs={{1,0},{2,1},{3,2},{4,3},{5,4},{6,5},{7,6},{9,8},{10,9},{11,10},{12... | collective-permute-start | bytes 2359304 | tf_op jit(solution)/shard_map/ppermute | solution.py:402
  34.0 11.6 %collective-permute-start.5 = (f32[2,256,256]{2,1,0:T(8,128)S(1)}, f32[2,256,256]{2,1,0:T(8,128)S(1)}, u32[]{:S(2)}, u32[]{:S(2)}) collective-permute-start(f32[2,256,256]{2,1,0:T(8,128)S(1)} %get-tuple-element.16), channel_id=1, source_target_pairs={{64,0},{128,64},{192,128},{65,1},{129,65},{193,129},{66,2},{130,66... | collective-permute-start | bytes 1572872 | tf_op jit(solution)/shard_map/ppermute | solution.py:402
  35.4 12.1 %collective-permute-start.4 = (f32[2,256,256]{2,1,0:T(8,128)S(1)}, f32[2,256,256]{2,1,0:T(8,128)S(1)}, u32[]{:S(2)}, u32[]{:S(2)}) collective-permute-start(f32[2,256,256]{2,1,0:T(8,128)S(1)} %get-tuple-element.16), channel_id=1, source_target_pairs={{0,64},{64,128},{128,192},{1,65},{65,129},{129,193},{2,66},{66,130... | collective-permute-start | bytes 1572872 | tf_op jit(solution)/shard_map/ppermute | solution.py:398
  45.7 14.5 %copy-start.8 = (f32[2,256,256]{2,1,0:T(8,128)}, f32[2,256,256]{2,1,0:T(8,128)S(1)}, u32[]{:S(2)}) copy-start(f32[2,256,256]{2,1,0:T(8,128)S(1)} %collective-permute-done.5.rest_6_.refs_4_) | copy-start | bytes 1572868
  47.4 12.7 %copy-start.9 = (f32[2,256,256]{2,1,0:T(8,128)}, f32[2,256,256]{2,1,0:T(8,128)S(1)}, u32[]{:S(2)}) copy-start(f32[2,256,256]{2,1,0:T(8,128)S(1)} %collective-permute-done.4.rest_5_.refs_5_) | copy-start | bytes 1572868
  47.4 5.1 %copy-start.6 = (f32[3,256,256]{2,1,0:T(8,128)}, f32[3,256,256]{2,1,0:T(8,128)S(1)}, u32[]{:S(2)}) copy-start(f32[3,256,256]{2,1,0:T(8,128)S(1)} %collective-permute-done.7.rest_8_.refs_1_) | copy-start | bytes 2359300
  49.5 3.2 %copy-start.7 = (f32[3,256,256]{2,1,0:T(8,128)}, f32[3,256,256]{2,1,0:T(8,128)S(1)}, u32[]{:S(2)}) copy-start(f32[3,256,256]{2,1,0:T(8,128)S(1)} %collective-permute-done.8.rest_9_.refs_0_) | copy-start | bytes 2359300
  49.5 2.9 %copy-start.5 = (f32[4,256,256]{2,1,0:T(8,128)}, f32[4,256,256]{2,1,0:T(8,128)S(1)}, u32[]{:S(2)}) copy-start(f32[4,256,256]{2,1,0:T(8,128)S(1)} %collective-permute-done.6.rest_7_.refs_6_) | copy-start | bytes 3145732
  52.5 26.0 %collective-permute-start.12 = (f32[14,256,256]{2,1,0:T(8,128)}, f32[14,256,256]{2,1,0:T(8,128)}, u32[]{:S(2)}, u32[]{:S(2)}) collective-permute-start(f32[14,256,256]{2,1,0:T(8,128)} %get-tuple-element.25), channel_id=1, source_target_pairs={{0,8},{8,0},{16,24},{24,16},{32,40},{40,32},{48,56},{56,48},{1,9},... | collective-permute-start | bytes 11010056 | tf_op jit(solution)/shard_map/ppermute | solution.py:382
  52.7 25.8 %collective-permute-start.9 = (f32[6,256,256]{2,1,0:T(8,128)}, f32[6,256,256]{2,1,0:T(8,128)S(1)}, u32[]{:S(2)}, u32[]{:S(2)}) collective-permute-start(f32[6,256,256]{2,1,0:T(8,128)} %get-tuple-element.22), channel_id=1, source_target_pairs={{8,16},{24,32},{40,48},{16,8},{32,24},{48,40},{9,17},{25,33},{41,4... | collective-permute-start | bytes 4718600 | tf_op jit(solution)/shard_map/ppermute | solution.py:408
  60.2 17.1 %collective-permute-start.10 = (f32[2,256,256]{2,1,0:T(8,128)}, f32[2,256,256]{2,1,0:T(8,128)S(1)}, u32[]{:S(2)}, u32[]{:S(2)}) collective-permute-start(f32[2,256,256]{2,1,0:T(8,128)} %get-tuple-element.23), channel_id=1, source_target_pairs={{0,1},{1,2},{2,3},{3,4},{4,5},{5,6},{6,7},{8,9},{9,10},{10,11},{11... | collective-permute-start | bytes 1572872 | tf_op jit(solution)/shard_map/ppermute | solution.py:398
  63.7 13.7 %collective-permute-start.11 = (f32[2,256,256]{2,1,0:T(8,128)}, f32[2,256,256]{2,1,0:T(8,128)S(1)}, u32[]{:S(2)}, u32[]{:S(2)}) collective-permute-start(f32[2,256,256]{2,1,0:T(8,128)} %get-tuple-element.24), channel_id=1, source_target_pairs={{1,0},{2,1},{3,2},{4,3},{5,4},{6,5},{7,6},{9,8},{10,9},{11,10},{12... | collective-permute-start | bytes 1572872 | tf_op jit(solution)/shard_map/ppermute | solution.py:402
  77.3 1.2 copy-start.11
  77.3 1.1 copy-start.12
  78.5 1.2 copy-start.10

commit v3 on v2

--- a/solution.py
+++ b/solution.py
@@ -20,8 +20,8 @@
 
 STAGES = (
     (
-        ("own", 4), ("o", 4), ("i", 4), ("ends-", 2), ("ends+", 2),
-        ("mids-", 2), ("mids+", 2), ("o2", 4), ("below2", 3), ("above2", 3),
+        ("own", 4), ("i", 4), ("ends-", 2), ("ends+", 2),
+        ("mids-", 2), ("mids+", 2), ("o2", 8), ("below2", 3), ("above2", 3),
     ),
     (("o3", 6), ("below3", 2), ("above3", 2), ("i3", 14)),
 )
@@ -43,7 +43,7 @@
         return ("mids" + sign, z - 1) if mid else ("ends" + sign, last)
     if inside:
         if dx == 0:
-            return (column, z)
+            return ("o2", 4 + z) if column == "o" else ("i", z)
         if mid:
             return (column + "3", 2 * side + z - 1)
         return ("o2", 2 * side + last) if column == "o" else ("i3", 10 + 2 * side + last)
@@ -121,11 +121,11 @@
     )(*(got[name] for name in names), *after)
 
 
-def listed(table_ref, codes_ref, chosen, begin):
+def listed(odd, table_ref, codes_ref, chosen, begin):
     taken = jnp.int32(0)
     for cell in range(CELLS):
         for at in range(cell * SLOTS, (cell + 1) * SLOTS):
-            entry = table_ref[27 * cell + codes_ref[at]]
+            entry = table_ref[odd, 27 * cell + codes_ref[cell, at - cell * SLOTS]]
 
             @pl.when(entry >= 0)
             def _(at=at, cell=cell, entry=entry, taken=taken):
@@ -173,8 +173,9 @@
     def fetch(at, n):
         return pltpu.make_async_copy(tiles_ref.at[at], tile.at[n], tile_sem.at[n])
 
-    taken = listed(table_ref, codes_ref, chosen, lambda at, n: fetch(at, n).start())
-    list_ref[0, ROOM - 1] = listed(later_ref, codes_ref, list_ref, lambda at, n: None)
+    odd = lax.axis_index("gy") % 2
+    taken = listed(odd, table_ref, codes_ref, chosen, lambda at, n: fetch(at, n).start())
+    list_ref[0, ROOM - 1] = listed(odd, later_ref, codes_ref, list_ref, lambda at, n: None)
     for copy in copies:
         copy.wait()
     for cell in range(CELLS):
@@ -239,9 +240,9 @@
 SLOT_ROOM = CELLS * SLOTS + GROUP
 
 
-def apply(odd, codes, tiles, got):
+def apply(codes, tiles, got):
     early, late = STAGES
-    tables = [jnp.where(odd, jnp.asarray(t[1]), jnp.asarray(t[0])) for t in map(lookup, STAGES)]
+    tables = [jnp.asarray(lookup(stage)) for stage in STAGES]
     counts = tuple(count for _, count in early)
     panel = jax.ShapeDtypeStruct((CELLS, SIDE, SIDE), F32)
     chosen = pltpu.SMEM((3, SLOT_ROOM), jnp.int32)
@@ -281,7 +282,7 @@
             pltpu.SemaphoreType.DMA((SLOT_ROOM,)),
             pltpu.SemaphoreType.DMA((CELLS + 1,)),
         ],
-        compiler_params=params,
+        compiler_params=pltpu.CompilerParams(vmem_limit_bytes=59_400_000),
         cost_estimate=cost,
         name="apply_late",
     )(left, tiles, part, *(got[name] for name, _ in late))
@@ -372,7 +373,7 @@
             pltpu.VMEM(panel, F32),
             pltpu.SemaphoreType.DMA((CELLS + 1,)),
         ],
-        compiler_params=pltpu.CompilerParams(vmem_limit_bytes=62_488_000),
+        compiler_params=pltpu.CompilerParams(vmem_limit_bytes=32 << 20),
         name="factorise",
     )(gram, filtered)
 
@@ -411,25 +412,24 @@
 def per_device(panel, tiles, codes):
     top = CELLS - 1
     own = panel[0, 0]
-    odd = lax.axis_index("gy") % 2 == 1
     tiles = tiles.reshape(CELLS * SLOTS, SIDE, SIDE)
-    codes = codes.reshape(CELLS * SLOTS)
-
-    ends = jnp.concatenate([own[:1], own[top:]], axis=0)
-    got = {"own": own}
+    codes = codes[0, 0]
+
+    first, last = own[:1], own[top:]
+    ends = jnp.concatenate([first, last], axis=0)
+    got = {"own": own, "first": first, "last": last, "between": own[1:top]}
     got["ends-"], got["ends+"] = up(ends, "gx"), down(ends, "gx")
-    got["o"] = across(own)
     got["i"] = flip(own, "gy", 1)
 
     sides, tops, bottoms, mids = pack(
         got,
         [
-            [("ends-", 0, 2), ("ends+", 0, 2)],
-            [("own", top, 1), ("ends-", 1, 1), ("ends+", 1, 1)],
-            [("own", 0, 1), ("ends-", 0, 1), ("ends+", 0, 1)],
-            [("own", 1, 2)],
+            [("ends-", 0, 2), ("ends+", 0, 2), ("first", 0, 1), ("between", 0, 2), ("last", 0, 1)],
+            [("last", 0, 1), ("ends-", 1, 1), ("ends+", 1, 1)],
+            [("first", 0, 1), ("ends-", 0, 1), ("ends+", 0, 1)],
+            [("between", 0, 2)],
         ],
-        after=(got["o"], got["i"]),
+        after=(got["i"],),
     )
     got["o2"] = across(sides)
     got["below2"], got["above2"] = up(tops, "gz"), down(bottoms, "gz")
@@ -451,7 +451,7 @@
     got["below3"], got["above3"] = up(tops, "gz"), down(bottoms, "gz")
     got["i3"] = flip(inner, "gy", 1)
 
-    filtered, gram = apply(odd, codes, tiles, got)
+    filtered, gram = apply(codes, tiles, got)
     devices = lax.axis_size("gx") * lax.axis_size("gy") * lax.axis_size("gz")
     bands, factor = factorise(summed(gram), filtered, CELLS * SIDE * devices)
     return bands.reshape(panel.shape), factor

time: 151 us -> 146 us (0.967)
  starting transfers between devices: 37.1 us -> 31 us
  waiting for transfers between devices: 21.8 us -> 26.8 us
  local copies, waits for them, and re-layouts: 5.09 us -> 3.36 us
    ppermute x3 -> x2, starting transfers between devices: 12.7 us -> 5.86 us  [across(): return lax.ppermute(values, 'gy', pairs + [(j, i) for i, j in pairs])]
    ppermute x4, waiting for transfers between devices: 17.1 us -> 22.9 us  [down(): lax.ppermute(values, axis, [(i + 1, i) for i in range(lax.axis_size(axis)...]
    pallas_call x1, Pallas kernels: 13.7 us -> 11.9 us  [factorise(): pl.pallas_call(functools.partial(factor_kernel, total), out_shape=(jax.Sh...]
    unnamed x36 -> x22, local copies, waits for them, and re-layouts: 3.34 us -> 2.24 us
  transfers between devices with their start and end apart: 13 -> 12, of which waited for: 6 -> 7; matrix products, arithmetic and copies ran while one was open for 2% -> 1% of each run, Pallas kernels for 7% -> 8%
where the time goes in v3:
time: 146 us
  blocking collectives  46.9 us (32%)
  Pallas kernels  36.5 us (25%)
  starting transfers between devices  31 us (21%)
  waiting for transfers between devices  26.8 us (18%)
  local copies, waits for them, and re-layouts  3.36 us (2%)
    all_to_all x3, blocking collectives, exchange(): return lax.all_to_all(pieces, axes, 0, 0).reshape(pieces.shape)  46.9 us
    ppermute x4, waiting for transfers between devices, down(): lax.ppermute(values, axis, [(i + 1, i) for i in range(lax.axis_size(axis)...  22.9 us
    ppermute x4, starting transfers between devices, up(): lax.ppermute(values, axis, [(i, i + 1) for i in range(lax.axis_size(axis)...  16.7 us
    pallas_call x1, Pallas kernels, factorise(): pl.pallas_call(functools.partial(factor_kernel, total), out_shape=(jax.Sh...  11.9 us
    pallas_call x1, Pallas kernels, apply(): pl.pallas_call(functools.partial(early_kernel, counts), out_shape=(panel,...  11.1 us
    pallas_call x1, Pallas kernels, apply(): pl.pallas_call(functools.partial(late_kernel, counts), out_shape=(panel,...  10.3 us
    ppermute x2, starting transfers between devices, across(): return lax.ppermute(values, 'gy', pairs + [(j, i) for i, j in pairs])  5.86 us
    ppermute x4, starting transfers between devices, down(): lax.ppermute(values, axis, [(i + 1, i) for i in range(lax.axis_size(axis)...  5.16 us
  transfers between devices with their start and end apart: 12, of which 7 were waited for; matrix products, arithmetic and copies ran while one was open for 1% of the time, Pallas kernels for 8%

profile of v3, /device:TPU:1, one launch (start us, length us, event | category | flops | bytes accessed | tf_op | source)
XLA Modules:
  0.0 145.7 jit_solution(2105789189441591163)
XLA Ops:
  0.6 0.0 copy-start.9
  0.6 3.3 %collective-permute-start = (f32[4,256,256]{2,1,0:T(8,128)}, f32[4,256,256]{2,1,0:T(8,128)S(1)}, u32[]{:S(2)}, u32[]{:S(2)}) collective-permute-start(f32[4,256,256]{2,1,0:T(8,128)} %bitcast.15), channel_id=1, source_target_pairs={{0,8},{8,0},{16,24},{24,16},{32,40},{40,32},{48,56},{56,48},{1,9},... | collective-permute-start | bytes 3145736 | tf_op jit(solution)/shard_map/ppermute | solution.py:383
  4.0 1.1 slice_bitcast_fusion.2
  5.1 1.3 collective-permute-start.2
  6.4 4.0 %collective-permute-start.1 = (f32[2,256,256]{2,1,0:T(8,128)S(1)}, f32[2,256,256]{2,1,0:T(8,128)S(1)}, u32[]{:S(2)}, u32[]{:S(2)}) collective-permute-start(f32[2,256,256]{2,1,0:T(8,128)S(1)} %pad_maximum_fusion), channel_id=1, source_target_pairs={{0,64},{64,128},{128,192},{1,65},{65,129},{129,193},{2,66},{66,130... | collective-permute-start | bytes 1572872 | tf_op jit(solution)/shard_map/ppermute | solution.py:399
  10.4 0.0 copy-done.9
  10.5 10.0 %collective-permute-done.2.refs_1_.rest_3_.refs_2_ = f32[2,256,256]{2,1,0:T(8,128)S(1)} collective-permute-done((f32[2,256,256]{2,1,0:T(8,128)S(1)}, f32[2,256,256]{2,1,0:T(8,128)S(1)}, u32[]{:S(2)}, u32[]{:S(2)}) %collective-permute-start.2) | collective-permute-done | bytes 524320 | tf_op jit(solution)/shard_map/ppermute | solution.py:403
  20.5 0.0 copy-start.1
  20.5 0.9 collective-permute-done.1.refs_2_.rest_2_.refs_3_
  21.3 0.0 copy-start.2
  21.3 0.0 collective-permute-done.refs_5_.rest_1_
  21.3 0.0 copy-start.3
  21.3 0.4 pack.2
  21.8 2.5 %collective-permute-start.5 = (f32[8,256,256]{2,1,0:T(8,128)S(1)}, f32[8,256,256]{2,1,0:T(8,128)S(1)}, u32[]{:S(2)}, u32[]{:S(2)}) collective-permute-start(f32[8,256,256]{2,1,0:T(8,128)S(1)} %get-tuple-element.17), channel_id=1, source_target_pairs={{8,16},{24,32},{40,48},{16,8},{32,24},{48,40},{9,17},{25,33},{41,4... | collective-permute-start | bytes 6291464 | tf_op jit(solution)/shard_map/ppermute | solution.py:409
  24.3 3.6 %collective-permute-start.6 = (f32[3,256,256]{2,1,0:T(8,128)S(1)}, f32[3,256,256]{2,1,0:T(8,128)S(1)}, u32[]{:S(2)}, u32[]{:S(2)}) collective-permute-start(f32[3,256,256]{2,1,0:T(8,128)S(1)} %get-tuple-element.18), channel_id=1, source_target_pairs={{0,1},{1,2},{2,3},{3,4},{4,5},{5,6},{6,7},{8,9},{9,10},{10,11},{11... | collective-permute-start | bytes 2359304 | tf_op jit(solution)/shard_map/ppermute | solution.py:399
  27.9 1.3 collective-permute-start.7
  29.2 1.3 collective-permute-start.4
  30.5 4.8 %collective-permute-start.3 = (f32[2,256,256]{2,1,0:T(8,128)S(1)}, f32[2,256,256]{2,1,0:T(8,128)S(1)}, u32[]{:S(2)}, u32[]{:S(2)}) collective-permute-start(f32[2,256,256]{2,1,0:T(8,128)S(1)} %get-tuple-element.16), channel_id=1, source_target_pairs={{0,64},{64,128},{128,192},{1,65},{65,129},{129,193},{2,66},{66,130... | collective-permute-start | bytes 1572872 | tf_op jit(solution)/shard_map/ppermute | solution.py:399
  35.3 8.7 %collective-permute-done.4.rest_5_.refs_4_ = f32[2,256,256]{2,1,0:T(8,128)S(1)} collective-permute-done((f32[2,256,256]{2,1,0:T(8,128)S(1)}, f32[2,256,256]{2,1,0:T(8,128)S(1)}, u32[]{:S(2)}, u32[]{:S(2)}) %collective-permute-start.4) | collective-permute-done | bytes 524320 | tf_op jit(solution)/shard_map/ppermute | solution.py:403
  44.0 0.0 copy-start.6
  44.0 1.5 %collective-permute-done.3.rest_4_.refs_5_ = f32[2,256,256]{2,1,0:T(8,128)S(1)} collective-permute-done((f32[2,256,256]{2,1,0:T(8,128)S(1)}, f32[2,256,256]{2,1,0:T(8,128)S(1)}, u32[]{:S(2)}, u32[]{:S(2)}) %collective-permute-start.3) | collective-permute-done | bytes 524320 | tf_op jit(solution)/shard_map/ppermute | solution.py:399
  45.4 0.0 copy-start.7
  45.4 0.0 collective-permute-done.6.rest_7_.refs_1_
  45.4 0.0 copy-done.3
  45.4 0.0 copy-start.4
  45.4 2.1 %collective-permute-done.7.rest_8_.refs_0_ = f32[3,256,256]{2,1,0:T(8,128)S(1)} collective-permute-done((f32[3,256,256]{2,1,0:T(8,128)S(1)}, f32[3,256,256]{2,1,0:T(8,128)S(1)}, u32[]{:S(2)}, u32[]{:S(2)}) %collective-permute-start.7) | collective-permute-done | bytes 786464 | tf_op jit(solution)/shard_map/ppermute | solution.py:403
  47.5 0.0 copy-start.5
  47.5 1.6 %collective-permute-done.5.rest_6_.refs_6_ = f32[8,256,256]{2,1,0:T(8,128)S(1)} collective-permute-done((f32[8,256,256]{2,1,0:T(8,128)S(1)}, f32[8,256,256]{2,1,0:T(8,128)S(1)}, u32[]{:S(2)}, u32[]{:S(2)}) %collective-permute-start.5) | collective-permute-done | bytes 2097184 | tf_op jit(solution)/shard_map/ppermute | solution.py:409
  49.1 0.0 copy-start
  49.1 2.8 %pack.3 = (f32[6,256,256]{2,1,0:T(8,128)}, f32[2,256,256]{2,1,0:T(8,128)}, f32[2,256,256]{2,1,0:T(8,128)}, f32[14,256,256]{2,1,0:T(8,128)}) custom-call(f32[3,256,256]{2,1,0:T(8,128)S(1)} %collective-permute-done.7.rest_8_.refs_0_, f32[3,256,256]{2,1,0:T(8,128)S(1)} %collective-permute-done.6.rest_7_.refs_1_, ...), custom_call_target="tpu_custom_call" | custom-call | tf_op jit(solution)/shard_map/pack/pallas_call | solution.py:110
  51.9 0.0 copy-done.1
  51.9 0.0 copy-done.2
  51.9 0.0 copy-done.6
  51.9 0.0 copy-done.7
  52.0 0.0 copy-done.4
  52.0 0.0 copy-done.5
  52.0 0.4 copy-done
  52.4 0.0 collective-permute-start.11
  52.4 3.3 %collective-permute-start.8 = (f32[6,256,256]{2,1,0:T(8,128)}, f32[6,256,256]{2,1,0:T(8,128)}, u32[]{:S(2)}, u32[]{:S(2)}) collective-permute-start(f32[6,256,256]{2,1,0:T(8,128)} %get-tuple-element.22), channel_id=1, source_target_pairs={{8,16},{24,32},{40,48},{16,8},{32,24},{48,40},{9,17},{25,33},{41,4... | collective-permute-start | bytes 4718600 | tf_op jit(solution)/shard_map/ppermute | solution.py:409
  55.7 4.3 %collective-permute-start.9 = (f32[2,256,256]{2,1,0:T(8,128)}, f32[2,256,256]{2,1,0:T(8,128)}, u32[]{:S(2)}, u32[]{:S(2)}) collective-permute-start(f32[2,256,256]{2,1,0:T(8,128)} %get-tuple-element.23), channel_id=1, source_target_pairs={{0,1},{1,2},{2,3},{3,4},{4,5},{5,6},{6,7},{8,9},{9,10},{10,11},{11... | collective-permute-start | bytes 1572872 | tf_op jit(solution)/shard_map/ppermute | solution.py:399
  60.0 1.3 collective-permute-start.10
  61.3 11.1 %apply_early.1 = (f32[4,256,256]{2,1,0:T(8,128)}, s32[3,48]{1,0:T(4,128)}) custom-call(s32[2,108]{1,0:T(2,128)} %constant.6.clone.table_ref, s32[2,108]{1,0:T(2,128)} %constant.7.clone.later_ref, s32[4,10]{1,0:T(4,128)} %bitcast.18, f32[40,256,256]{2,1,0:T(8,128)} %bitcast.13, f32[4,256,256]{2,1,0:T(8,128)} %bitcast.16, f32[4,256,256]{2,1,0:T(8,128)} %copy-done.3, ...), custom_call_target="tpu_custom_call" | custom-call | flops 1342177280 | bytes 12582912 | tf_op jit(solution)/shard_map/apply_early/pallas_call | solution.py:254
  72.4 0.0 collective-permute-done.9.rest_1_
  72.4 2.1 %collective-permute-done.10.rest_2_ = f32[2,256,256]{2,1,0:T(8,128)} collective-permute-done((f32[2,256,256]{2,1,0:T(8,128)}, f32[2,256,256]{2,1,0:T(8,128)}, u32[]{:S(2)}, u32[]{:S(2)}) %collective-permute-start.10) | collective-permute-done | bytes 524320 | tf_op jit(solution)/shard_map/ppermute | solution.py:403
  74.5 0.0 collective-permute-done.8.rest_0_
  74.5 0.0 collective-permute-done.11.rest_3_
  74.5 0.0 copy-start.10
  74.5 1.8 %copy-done.10 = f32[14,256,256]{2,1,0:T(8,128)} copy-done((f32[14,256,256]{2,1,0:T(8,128)}, f32[14,256,256]{2,1,0:T(8,128)S(1)}, u32[]{:S(2)}) %copy-start.10) | copy-done | bytes 3670040
  76.3 10.3 %apply_late.1 = (f32[4,256,256]{2,1,0:T(8,128)}, f32[256,256]{1,0:T(8,128)}) custom-call(s32[3,48]{1,0:T(4,128)} %get-tuple-element.20.list_ref, f32[40,256,256]{2,1,0:T(8,128)} %bitcast.14, f32[4,256,256]{2,1,0:T(8,128)} %get-tuple-element.21.before_ref, f32[6,256,256]{2,1,0:T(8,128)} %collective-permute-done.8.rest_0_, ...), custom_call_target="tpu_custom_call" | custom-call | flops 1342177280 | bytes 12582912 | tf_op jit(solution)/shard_map/apply_late/pallas_call | solution.py:271
  86.6 0.0 copy-start.8
  86.6 18.4 %all_to_all.15 = f32[32,8,256]{2,1,0:T(8,128)S(1)} all-to-all(f32[32,8,256]{2,1,0:T(8,128)} %bitcast.17), channel_id=1, replica_groups=mesh['gx'=4,'gy'=8,'gz'=8] {'gx','gy'}, dimensions={0} | all-to-all | bytes 524288 | tf_op jit(solution)/shard_map/all_to_all | solution.py:387
  105.1 14.5 %all_to_all.16 = f32[8,8,256]{2,1,0:T(8,128)S(1)} all-to-all(f32[8,8,256]{2,1,0:T(8,128)S(1)} %broadcast_in_dim.6), channel_id=1, replica_groups=mesh['gx'=4,'gy'=8,'gz'=8] {'gz'}, dimensions={0} | all-to-all | bytes 131072 | tf_op jit(solution)/shard_map/all_to_all | solution.py:387
  119.7 13.9 %all_to_all.17 = f32[32,8,256]{2,1,0:T(8,128)S(1)} all-to-all(f32[32,8,256]{2,1,0:T(8,128)S(1)} %broadcast_in_dim.7), channel_id=1, replica_groups=mesh['gx'=4,'gy'=8,'gz'=8] {'gx','gy'}, dimensions={0} | all-to-all | bytes 524288 | tf_op jit(solution)/shard_map/all_to_all | solution.py:387
  133.6 0.0 copy-done.8
  133.6 11.9 %factorise.1 = (f32[4,256,256]{2,1,0:T(8,128)}, f32[256,256]{1,0:T(8,128)}) custom-call(f32[256,256]{1,0:T(8,128)S(1)} %bitcast.12, f32[4,256,256]{2,1,0:T(8,128)S(1)} %copy-done.8), custom_call_target="tpu_custom_call" | custom-call | tf_op jit(solution)/shard_map/factorise/pallas_call | solution.py:365
  (6 shorter events, 0.1 us)
Async XLA Ops:
  0.6 9.8 %copy-start.9 = (f32[1,1,4,256,256]{4,3,2,1,0:T(8,128)S(1)}, f32[1,1,4,256,256]{4,3,2,1,0:T(8,128)}, u32[]{:S(2)}) copy-start(f32[1,1,4,256,256]{4,3,2,1,0:T(8,128)} %param.5) | copy-start | bytes 3145732
  0.6 20.7 %collective-permute-start = (f32[4,256,256]{2,1,0:T(8,128)}, f32[4,256,256]{2,1,0:T(8,128)S(1)}, u32[]{:S(2)}, u32[]{:S(2)}) collective-permute-start(f32[4,256,256]{2,1,0:T(8,128)} %bitcast.15), channel_id=1, source_target_pairs={{0,8},{8,0},{16,24},{24,16},{32,40},{40,32},{48,56},{56,48},{1,9},... | collective-permute-start | bytes 3145736 | tf_op jit(solution)/shard_map/ppermute | solution.py:383
  5.1 15.4 %collective-permute-start.2 = (f32[2,256,256]{2,1,0:T(8,128)S(1)}, f32[2,256,256]{2,1,0:T(8,128)S(1)}, u32[]{:S(2)}, u32[]{:S(2)}) collective-permute-start(f32[2,256,256]{2,1,0:T(8,128)S(1)} %pad_maximum_fusion), channel_id=1, source_target_pairs={{64,0},{128,64},{192,128},{65,1},{129,65},{193,129},{66,2},{130,66... | collective-permute-start | bytes 1572872 | tf_op jit(solution)/shard_map/ppermute | solution.py:403
  6.4 14.9 %collective-permute-start.1 = (f32[2,256,256]{2,1,0:T(8,128)S(1)}, f32[2,256,256]{2,1,0:T(8,128)S(1)}, u32[]{:S(2)}, u32[]{:S(2)}) collective-permute-start(f32[2,256,256]{2,1,0:T(8,128)S(1)} %pad_maximum_fusion), channel_id=1, source_target_pairs={{0,64},{64,128},{128,192},{1,65},{65,129},{129,193},{2,66},{66,130... | collective-permute-start | bytes 1572872 | tf_op jit(solution)/shard_map/ppermute | solution.py:399
  20.5 31.5 %copy-start.1 = (f32[2,256,256]{2,1,0:T(8,128)}, f32[2,256,256]{2,1,0:T(8,128)S(1)}, u32[]{:S(2)}) copy-start(f32[2,256,256]{2,1,0:T(8,128)S(1)} %collective-permute-done.2.refs_1_.rest_3_.refs_2_) | copy-start | bytes 1572868
  21.3 30.6 %copy-start.2 = (f32[2,256,256]{2,1,0:T(8,128)}, f32[2,256,256]{2,1,0:T(8,128)S(1)}, u32[]{:S(2)}) copy-start(f32[2,256,256]{2,1,0:T(8,128)S(1)} %collective-permute-done.1.refs_2_.rest_2_.refs_3_) | copy-start | bytes 1572868
  21.3 24.1 %copy-start.3 = (f32[4,256,256]{2,1,0:T(8,128)}, f32[4,256,256]{2,1,0:T(8,128)S(1)}, u32[]{:S(2)}) copy-start(f32[4,256,256]{2,1,0:T(8,128)S(1)} %collective-permute-done.refs_5_.rest_1_) | copy-start | bytes 3145732
  21.8 27.4 %collective-permute-start.5 = (f32[8,256,256]{2,1,0:T(8,128)S(1)}, f32[8,256,256]{2,1,0:T(8,128)S(1)}, u32[]{:S(2)}, u32[]{:S(2)}) collective-permute-start(f32[8,256,256]{2,1,0:T(8,128)S(1)} %get-tuple-element.17), channel_id=1, source_target_pairs={{8,16},{24,32},{40,48},{16,8},{32,24},{48,40},{9,17},{25,33},{41,4... | collective-permute-start | bytes 6291464 | tf_op jit(solution)/shard_map/ppermute | solution.py:409
  24.3 21.1 %collective-permute-start.6 = (f32[3,256,256]{2,1,0:T(8,128)S(1)}, f32[3,256,256]{2,1,0:T(8,128)S(1)}, u32[]{:S(2)}, u32[]{:S(2)}) collective-permute-start(f32[3,256,256]{2,1,0:T(8,128)S(1)} %get-tuple-element.18), channel_id=1, source_target_pairs={{0,1},{1,2},{2,3},{3,4},{4,5},{5,6},{6,7},{8,9},{9,10},{10,11},{11... | collective-permute-start | bytes 2359304 | tf_op jit(solution)/shard_map/ppermute | solution.py:399
  27.9 19.6 %collective-permute-start.7 = (f32[3,256,256]{2,1,0:T(8,128)S(1)}, f32[3,256,256]{2,1,0:T(8,128)S(1)}, u32[]{:S(2)}, u32[]{:S(2)}) collective-permute-start(f32[3,256,256]{2,1,0:T(8,128)S(1)} %get-tuple-element.19), channel_id=1, source_target_pairs={{1,0},{2,1},{3,2},{4,3},{5,4},{6,5},{7,6},{9,8},{10,9},{11,10},{12... | collective-permute-start | bytes 2359304 | tf_op jit(solution)/shard_map/ppermute | solution.py:403
  29.2 14.8 %collective-permute-start.4 = (f32[2,256,256]{2,1,0:T(8,128)S(1)}, f32[2,256,256]{2,1,0:T(8,128)S(1)}, u32[]{:S(2)}, u32[]{:S(2)}) collective-permute-start(f32[2,256,256]{2,1,0:T(8,128)S(1)} %get-tuple-element.16), channel_id=1, source_target_pairs={{64,0},{128,64},{192,128},{65,1},{129,65},{193,129},{66,2},{130,66... | collective-permute-start | bytes 1572872 | tf_op jit(solution)/shard_map/ppermute | solution.py:403
  30.5 14.9 %collective-permute-start.3 = (f32[2,256,256]{2,1,0:T(8,128)S(1)}, f32[2,256,256]{2,1,0:T(8,128)S(1)}, u32[]{:S(2)}, u32[]{:S(2)}) collective-permute-start(f32[2,256,256]{2,1,0:T(8,128)S(1)} %get-tuple-element.16), channel_id=1, source_target_pairs={{0,64},{64,128},{128,192},{1,65},{65,129},{129,193},{2,66},{66,130... | collective-permute-start | bytes 1572872 | tf_op jit(solution)/shard_map/ppermute | solution.py:399
  44.0 8.0 %copy-start.6 = (f32[2,256,256]{2,1,0:T(8,128)}, f32[2,256,256]{2,1,0:T(8,128)S(1)}, u32[]{:S(2)}) copy-start(f32[2,256,256]{2,1,0:T(8,128)S(1)} %collective-permute-done.4.rest_5_.refs_4_) | copy-start | bytes 1572868
  45.4 6.5 %copy-start.7 = (f32[2,256,256]{2,1,0:T(8,128)}, f32[2,256,256]{2,1,0:T(8,128)S(1)}, u32[]{:S(2)}) copy-start(f32[2,256,256]{2,1,0:T(8,128)S(1)} %collective-permute-done.3.rest_4_.refs_5_) | copy-start | bytes 1572868
  45.4 6.5 %copy-start.4 = (f32[3,256,256]{2,1,0:T(8,128)}, f32[3,256,256]{2,1,0:T(8,128)S(1)}, u32[]{:S(2)}) copy-start(f32[3,256,256]{2,1,0:T(8,128)S(1)} %collective-permute-done.6.rest_7_.refs_1_) | copy-start | bytes 2359300
  47.5 4.5 %copy-start.5 = (f32[3,256,256]{2,1,0:T(8,128)}, f32[3,256,256]{2,1,0:T(8,128)S(1)}, u32[]{:S(2)}) copy-start(f32[3,256,256]{2,1,0:T(8,128)S(1)} %collective-permute-done.7.rest_8_.refs_0_) | copy-start | bytes 2359300
  49.1 3.3 %copy-start = (f32[8,256,256]{2,1,0:T(8,128)}, f32[8,256,256]{2,1,0:T(8,128)S(1)}, u32[]{:S(2)}) copy-start(f32[8,256,256]{2,1,0:T(8,128)S(1)} %collective-permute-done.5.rest_6_.refs_6_) | copy-start | bytes 6291460
  52.4 22.1 %collective-permute-start.11 = (f32[14,256,256]{2,1,0:T(8,128)}, f32[14,256,256]{2,1,0:T(8,128)S(1)}, u32[]{:S(2)}, u32[]{:S(2)}) collective-permute-start(f32[14,256,256]{2,1,0:T(8,128)} %get-tuple-element.25), channel_id=1, source_target_pairs={{0,8},{8,0},{16,24},{24,16},{32,40},{40,32},{48,56},{56,48},{1,9},... | collective-permute-start | bytes 11010056 | tf_op jit(solution)/shard_map/ppermute | solution.py:383
  52.4 22.1 %collective-permute-start.8 = (f32[6,256,256]{2,1,0:T(8,128)}, f32[6,256,256]{2,1,0:T(8,128)}, u32[]{:S(2)}, u32[]{:S(2)}) collective-permute-start(f32[6,256,256]{2,1,0:T(8,128)} %get-tuple-element.22), channel_id=1, source_target_pairs={{8,16},{24,32},{40,48},{16,8},{32,24},{48,40},{9,17},{25,33},{41,4... | collective-permute-start | bytes 4718600 | tf_op jit(solution)/shard_map/ppermute | solution.py:409
  55.7 16.7 %collective-permute-start.9 = (f32[2,256,256]{2,1,0:T(8,128)}, f32[2,256,256]{2,1,0:T(8,128)}, u32[]{:S(2)}, u32[]{:S(2)}) collective-permute-start(f32[2,256,256]{2,1,0:T(8,128)} %get-tuple-element.23), channel_id=1, source_target_pairs={{0,1},{1,2},{2,3},{3,4},{4,5},{5,6},{6,7},{8,9},{9,10},{10,11},{11... | collective-permute-start | bytes 1572872 | tf_op jit(solution)/shard_map/ppermute | solution.py:399
  60.0 14.5 %collective-permute-start.10 = (f32[2,256,256]{2,1,0:T(8,128)}, f32[2,256,256]{2,1,0:T(8,128)}, u32[]{:S(2)}, u32[]{:S(2)}) collective-permute-start(f32[2,256,256]{2,1,0:T(8,128)} %get-tuple-element.24), channel_id=1, source_target_pairs={{1,0},{2,1},{3,2},{4,3},{5,4},{6,5},{7,6},{9,8},{10,9},{11,10},{12... | collective-permute-start | bytes 1572872 | tf_op jit(solution)/shard_map/ppermute | solution.py:403
  74.5 1.8 %copy-start.10 = (f32[14,256,256]{2,1,0:T(8,128)}, f32[14,256,256]{2,1,0:T(8,128)S(1)}, u32[]{:S(2)}) copy-start(f32[14,256,256]{2,1,0:T(8,128)S(1)} %collective-permute-done.11.rest_3_) | copy-start | bytes 11010052
  86.6 47.0 %copy-start.8 = (f32[4,256,256]{2,1,0:T(8,128)S(1)}, f32[4,256,256]{2,1,0:T(8,128)}, u32[]{:S(2)}) copy-start(f32[4,256,256]{2,1,0:T(8,128)} %get-tuple-element.27.filtered_ref) | copy-start | bytes 3145732

commit v4 on v3

--- a/solution.py
+++ b/solution.py
@@ -282,7 +282,7 @@
             pltpu.SemaphoreType.DMA((SLOT_ROOM,)),
             pltpu.SemaphoreType.DMA((CELLS + 1,)),
         ],
-        compiler_params=pltpu.CompilerParams(vmem_limit_bytes=59_400_000),
+        compiler_params=pltpu.CompilerParams(vmem_limit_bytes=53_500_000),
         cost_estimate=cost,
         name="apply_late",
     )(left, tiles, part, *(got[name] for name, _ in late))

time: 146 us -> 145 us (level)
  Pallas kernels: 36.5 us -> 34.8 us
  blocking collectives: 46.9 us -> 48.5 us
    pallas_call x1, Pallas kernels: 10.3 us -> 6.98 us  [apply(): pl.pallas_call(functools.partial(late_kernel, counts), out_shape=(panel,...]
    ppermute x4, waiting for transfers between devices: 22.9 us -> 20.7 us  [down(): lax.ppermute(values, axis, [(i + 1, i) for i in range(lax.axis_size(axis)...]
    pallas_call x1, Pallas kernels: 11.1 us -> 12.8 us  [apply(): pl.pallas_call(functools.partial(early_kernel, counts), out_shape=(panel,...]
    all_to_all x3, blocking collectives: 46.9 us -> 48.5 us  [exchange(): return lax.all_to_all(pieces, axes, 0, 0).reshape(pieces.shape)]
  transfers between devices with their start and end apart: 12 -> 12, of which waited for: 7 -> 7; matrix products, arithmetic and copies ran while one was open for 1% -> 1% of each run, Pallas kernels for 8% -> 9%
where the time goes in v4:
time: 145 us; the launch traced here: 144 us
  blocking collectives  48.5 us (33%)
  Pallas kernels  34.8 us (24%)
  starting transfers between devices  30.3 us (21%)
  waiting for transfers between devices  25.6 us (18%)
  local copies, waits for them, and re-layouts  3.56 us (2%)
    all_to_all x3, blocking collectives, exchange(): return lax.all_to_all(pieces, axes, 0, 0).reshape(pieces.shape)  48.5 us
    ppermute x4, waiting for transfers between devices, down(): lax.ppermute(values, axis, [(i + 1, i) for i in range(lax.axis_size(axis)...  20.7 us
    ppermute x4, starting transfers between devices, up(): lax.ppermute(values, axis, [(i, i + 1) for i in range(lax.axis_size(axis)...  15.9 us
    pallas_call x1, Pallas kernels, apply(): pl.pallas_call(functools.partial(early_kernel, counts), out_shape=(panel,...  12.8 us
    pallas_call x1, Pallas kernels, factorise(): pl.pallas_call(functools.partial(factor_kernel, total), out_shape=(jax.Sh...  11.9 us
    pallas_call x1, Pallas kernels, apply(): pl.pallas_call(functools.partial(late_kernel, counts), out_shape=(panel,...  6.98 us
    ppermute x2, starting transfers between devices, across(): return lax.ppermute(values, 'gy', pairs + [(j, i) for i, j in pairs])  5.87 us
    ppermute x4, starting transfers between devices, down(): lax.ppermute(values, axis, [(i + 1, i) for i in range(lax.axis_size(axis)...  5.17 us
  transfers between devices with their start and end apart: 12, of which 7 were waited for; matrix products, arithmetic and copies ran while one was open for 1% of the time, Pallas kernels for 9%

profile of v4, /device:TPU:1, one launch (start us, length us, event | category | flops | bytes accessed | tf_op | source)
XLA Modules:
  0.0 143.9 jit_solution(9936565680204860914)
XLA Ops:
  0.6 0.0 copy-start.9
  0.6 3.3 %collective-permute-start = (f32[4,256,256]{2,1,0:T(8,128)}, f32[4,256,256]{2,1,0:T(8,128)S(1)}, u32[]{:S(2)}, u32[]{:S(2)}) collective-permute-start(f32[4,256,256]{2,1,0:T(8,128)} %bitcast.16), channel_id=1, source_target_pairs={{0,8},{8,0},{16,24},{24,16},{32,40},{40,32},{48,56},{56,48},{1,9},... | collective-permute-start | bytes 3145736 | tf_op jit(solution)/shard_map/ppermute | solution.py:383
  4.0 1.1 slice_bitcast_fusion.2
  5.1 1.3 collective-permute-start.2
  6.4 4.0 %collective-permute-start.1 = (f32[2,256,256]{2,1,0:T(8,128)S(1)}, f32[2,256,256]{2,1,0:T(8,128)S(1)}, u32[]{:S(2)}, u32[]{:S(2)}) collective-permute-start(f32[2,256,256]{2,1,0:T(8,128)S(1)} %pad_maximum_fusion), channel_id=1, source_target_pairs={{0,64},{64,128},{128,192},{1,65},{65,129},{129,193},{2,66},{66,130... | collective-permute-start | bytes 1572872 | tf_op jit(solution)/shard_map/ppermute | solution.py:399
  10.4 0.0 copy-done.9
  10.5 10.0 %collective-permute-done.2.refs_1_.rest_3_.refs_2_ = f32[2,256,256]{2,1,0:T(8,128)S(1)} collective-permute-done((f32[2,256,256]{2,1,0:T(8,128)S(1)}, f32[2,256,256]{2,1,0:T(8,128)S(1)}, u32[]{:S(2)}, u32[]{:S(2)}) %collective-permute-start.2) | collective-permute-done | bytes 524320 | tf_op jit(solution)/shard_map/ppermute | solution.py:403
  20.5 0.0 copy-start.1
  20.5 0.9 collective-permute-done.1.refs_2_.rest_2_.refs_3_
  21.3 0.0 copy-start.2
  21.3 0.0 collective-permute-done.refs_5_.rest_1_
  21.3 0.0 copy-start.3
  21.3 0.4 pack.2
  21.8 2.5 %collective-permute-start.5 = (f32[8,256,256]{2,1,0:T(8,128)S(1)}, f32[8,256,256]{2,1,0:T(8,128)S(1)}, u32[]{:S(2)}, u32[]{:S(2)}) collective-permute-start(f32[8,256,256]{2,1,0:T(8,128)S(1)} %get-tuple-element.17), channel_id=1, source_target_pairs={{8,16},{24,32},{40,48},{16,8},{32,24},{48,40},{9,17},{25,33},{41,4... | collective-permute-start | bytes 6291464 | tf_op jit(solution)/shard_map/ppermute | solution.py:409
  24.3 3.6 %collective-permute-start.6 = (f32[3,256,256]{2,1,0:T(8,128)S(1)}, f32[3,256,256]{2,1,0:T(8,128)S(1)}, u32[]{:S(2)}, u32[]{:S(2)}) collective-permute-start(f32[3,256,256]{2,1,0:T(8,128)S(1)} %get-tuple-element.18), channel_id=1, source_target_pairs={{0,1},{1,2},{2,3},{3,4},{4,5},{5,6},{6,7},{8,9},{9,10},{10,11},{11... | collective-permute-start | bytes 2359304 | tf_op jit(solution)/shard_map/ppermute | solution.py:399
  27.9 1.3 collective-permute-start.7
  29.2 1.3 collective-permute-start.4
  30.5 4.8 %collective-permute-start.3 = (f32[2,256,256]{2,1,0:T(8,128)S(1)}, f32[2,256,256]{2,1,0:T(8,128)S(1)}, u32[]{:S(2)}, u32[]{:S(2)}) collective-permute-start(f32[2,256,256]{2,1,0:T(8,128)S(1)} %get-tuple-element.16), channel_id=1, source_target_pairs={{0,64},{64,128},{128,192},{1,65},{65,129},{129,193},{2,66},{66,130... | collective-permute-start | bytes 1572872 | tf_op jit(solution)/shard_map/ppermute | solution.py:399
  35.3 8.7 %collective-permute-done.4.rest_5_.refs_4_ = f32[2,256,256]{2,1,0:T(8,128)S(1)} collective-permute-done((f32[2,256,256]{2,1,0:T(8,128)S(1)}, f32[2,256,256]{2,1,0:T(8,128)S(1)}, u32[]{:S(2)}, u32[]{:S(2)}) %collective-permute-start.4) | collective-permute-done | bytes 524320 | tf_op jit(solution)/shard_map/ppermute | solution.py:403
  44.0 0.0 copy-start.6
  44.0 1.5 %collective-permute-done.3.rest_4_.refs_5_ = f32[2,256,256]{2,1,0:T(8,128)S(1)} collective-permute-done((f32[2,256,256]{2,1,0:T(8,128)S(1)}, f32[2,256,256]{2,1,0:T(8,128)S(1)}, u32[]{:S(2)}, u32[]{:S(2)}) %collective-permute-start.3) | collective-permute-done | bytes 524320 | tf_op jit(solution)/shard_map/ppermute | solution.py:399
  45.4 0.0 copy-start.7
  45.4 0.0 collective-permute-done.6.rest_7_.refs_1_
  45.4 0.0 copy-done.3
  45.4 0.0 copy-start.4
  45.4 2.1 %collective-permute-done.7.rest_8_.refs_0_ = f32[3,256,256]{2,1,0:T(8,128)S(1)} collective-permute-done((f32[3,256,256]{2,1,0:T(8,128)S(1)}, f32[3,256,256]{2,1,0:T(8,128)S(1)}, u32[]{:S(2)}, u32[]{:S(2)}) %collective-permute-start.7) | collective-permute-done | bytes 786464 | tf_op jit(solution)/shard_map/ppermute | solution.py:403
  47.5 0.0 copy-start.5
  47.5 1.6 %collective-permute-done.5.rest_6_.refs_6_ = f32[8,256,256]{2,1,0:T(8,128)S(1)} collective-permute-done((f32[8,256,256]{2,1,0:T(8,128)S(1)}, f32[8,256,256]{2,1,0:T(8,128)S(1)}, u32[]{:S(2)}, u32[]{:S(2)}) %collective-permute-start.5) | collective-permute-done | bytes 2097184 | tf_op jit(solution)/shard_map/ppermute | solution.py:409
  49.1 0.0 copy-start
  49.1 2.7 %pack.3 = (f32[6,256,256]{2,1,0:T(8,128)}, f32[2,256,256]{2,1,0:T(8,128)}, f32[2,256,256]{2,1,0:T(8,128)}, f32[14,256,256]{2,1,0:T(8,128)}) custom-call(f32[3,256,256]{2,1,0:T(8,128)S(1)} %collective-permute-done.7.rest_8_.refs_0_, f32[3,256,256]{2,1,0:T(8,128)S(1)} %collective-permute-done.6.rest_7_.refs_1_, ...), custom_call_target="tpu_custom_call" | custom-call | tf_op jit(solution)/shard_map/pack/pallas_call | solution.py:110
  51.8 0.0 copy-done.1
  51.8 0.0 copy-done.2
  51.8 0.0 copy-done.6
  51.9 0.0 copy-done.7
  51.9 0.0 copy-done.4
  51.9 0.0 copy-done.5
  51.9 0.5 copy-done
  52.4 0.0 collective-permute-start.11
  52.4 3.3 %collective-permute-start.8 = (f32[6,256,256]{2,1,0:T(8,128)}, f32[6,256,256]{2,1,0:T(8,128)S(1)}, u32[]{:S(2)}, u32[]{:S(2)}) collective-permute-start(f32[6,256,256]{2,1,0:T(8,128)} %get-tuple-element.22), channel_id=1, source_target_pairs={{8,16},{24,32},{40,48},{16,8},{32,24},{48,40},{9,17},{25,33},{41,4... | collective-permute-start | bytes 4718600 | tf_op jit(solution)/shard_map/ppermute | solution.py:409
  55.7 3.5 %collective-permute-start.9 = (f32[2,256,256]{2,1,0:T(8,128)}, f32[2,256,256]{2,1,0:T(8,128)S(1)}, u32[]{:S(2)}, u32[]{:S(2)}) collective-permute-start(f32[2,256,256]{2,1,0:T(8,128)} %get-tuple-element.23), channel_id=1, source_target_pairs={{0,1},{1,2},{2,3},{3,4},{4,5},{5,6},{6,7},{8,9},{9,10},{10,11},{11... | collective-permute-start | bytes 1572872 | tf_op jit(solution)/shard_map/ppermute | solution.py:399
  59.3 1.3 collective-permute-start.10
  60.6 12.8 %apply_early.1 = (f32[4,256,256]{2,1,0:T(8,128)}, s32[3,48]{1,0:T(4,128)}) custom-call(s32[2,108]{1,0:T(2,128)} %constant.6.clone.table_ref, s32[2,108]{1,0:T(2,128)} %constant.7.clone.later_ref, s32[4,10]{1,0:T(4,128)} %bitcast.18, f32[40,256,256]{2,1,0:T(8,128)} %bitcast.14, f32[4,256,256]{2,1,0:T(8,128)} %bitcast.17, f32[4,256,256]{2,1,0:T(8,128)} %copy-done.3, ...), custom_call_target="tpu_custom_call" | custom-call | flops 1342177280 | bytes 12582912 | tf_op jit(solution)/shard_map/apply_early/pallas_call | solution.py:254
  73.3 0.0 collective-permute-done.9.rest_1_
  73.4 0.0 collective-permute-done.10.rest_2_
  73.4 1.0 collective-permute-done.8.rest_0_
  74.3 0.0 copy-start.10
  74.3 0.0 collective-permute-done.11.rest_3_
  74.3 1.2 copy-done.10
  75.5 0.0 copy-start.8
  75.6 0.7 copy-done.8
  76.2 7.0 %apply_late.1 = (f32[4,256,256]{2,1,0:T(8,128)S(1)}, f32[256,256]{1,0:T(8,128)S(1)}) custom-call(s32[3,48]{1,0:T(4,128)S(1)} %copy-done.8, f32[40,256,256]{2,1,0:T(8,128)} %bitcast.15, f32[4,256,256]{2,1,0:T(8,128)} %get-tuple-element.21.before_ref, f32[6,256,256]{2,1,0:T(8,128)} %copy-done.10, f32[2,256,256]{2,1,0:T(8,128)S(1)} %collective-permute-done.9.rest_1_, ...), custom_call_target="tpu_custom_call" | custom-call | flops 1342177280 | bytes 12582912 | tf_op jit(solution)/shard_map/apply_late/pallas_call | solution.py:271
  83.2 20.6 %all_to_all.15 = f32[32,8,256]{2,1,0:T(8,128)S(1)} all-to-all(f32[32,8,256]{2,1,0:T(8,128)S(1)} %bitcast.13), channel_id=1, replica_groups=mesh['gx'=4,'gy'=8,'gz'=8] {'gx','gy'}, dimensions={0} | all-to-all | bytes 524288 | tf_op jit(solution)/shard_map/all_to_all | solution.py:387
  103.8 14.0 %all_to_all.16 = f32[8,8,256]{2,1,0:T(8,128)S(1)} all-to-all(f32[8,8,256]{2,1,0:T(8,128)S(1)} %broadcast_in_dim.6), channel_id=1, replica_groups=mesh['gx'=4,'gy'=8,'gz'=8] {'gz'}, dimensions={0} | all-to-all | bytes 131072 | tf_op jit(solution)/shard_map/all_to_all | solution.py:387
  117.9 13.9 %all_to_all.17 = f32[32,8,256]{2,1,0:T(8,128)S(1)} all-to-all(f32[32,8,256]{2,1,0:T(8,128)S(1)} %broadcast_in_dim.7), channel_id=1, replica_groups=mesh['gx'=4,'gy'=8,'gz'=8] {'gx','gy'}, dimensions={0} | all-to-all | bytes 524288 | tf_op jit(solution)/shard_map/all_to_all | solution.py:387
  131.9 11.9 %factorise.1 = (f32[4,256,256]{2,1,0:T(8,128)}, f32[256,256]{1,0:T(8,128)}) custom-call(f32[256,256]{1,0:T(8,128)S(1)} %bitcast.12, f32[4,256,256]{2,1,0:T(8,128)S(1)} %get-tuple-element.27.filtered_ref), custom_call_target="tpu_custom_call" | custom-call | tf_op jit(solution)/shard_map/factorise/pallas_call | solution.py:365
  (6 shorter events, 0.1 us)
Async XLA Ops:
  0.6 9.8 %copy-start.9 = (f32[1,1,4,256,256]{4,3,2,1,0:T(8,128)S(1)}, f32[1,1,4,256,256]{4,3,2,1,0:T(8,128)}, u32[]{:S(2)}) copy-start(f32[1,1,4,256,256]{4,3,2,1,0:T(8,128)} %param.5) | copy-start | bytes 3145732
  0.6 20.7 %collective-permute-start = (f32[4,256,256]{2,1,0:T(8,128)}, f32[4,256,256]{2,1,0:T(8,128)S(1)}, u32[]{:S(2)}, u32[]{:S(2)}) collective-permute-start(f32[4,256,256]{2,1,0:T(8,128)} %bitcast.16), channel_id=1, source_target_pairs={{0,8},{8,0},{16,24},{24,16},{32,40},{40,32},{48,56},{56,48},{1,9},... | collective-permute-start | bytes 3145736 | tf_op jit(solution)/shard_map/ppermute | solution.py:383
  5.1 15.4 %collective-permute-start.2 = (f32[2,256,256]{2,1,0:T(8,128)S(1)}, f32[2,256,256]{2,1,0:T(8,128)S(1)}, u32[]{:S(2)}, u32[]{:S(2)}) collective-permute-start(f32[2,256,256]{2,1,0:T(8,128)S(1)} %pad_maximum_fusion), channel_id=1, source_target_pairs={{64,0},{128,64},{192,128},{65,1},{129,65},{193,129},{66,2},{130,66... | collective-permute-start | bytes 1572872 | tf_op jit(solution)/shard_map/ppermute | solution.py:403
  6.4 14.9 %collective-permute-start.1 = (f32[2,256,256]{2,1,0:T(8,128)S(1)}, f32[2,256,256]{2,1,0:T(8,128)S(1)}, u32[]{:S(2)}, u32[]{:S(2)}) collective-permute-start(f32[2,256,256]{2,1,0:T(8,128)S(1)} %pad_maximum_fusion), channel_id=1, source_target_pairs={{0,64},{64,128},{128,192},{1,65},{65,129},{129,193},{2,66},{66,130... | collective-permute-start | bytes 1572872 | tf_op jit(solution)/shard_map/ppermute | solution.py:399
  20.5 31.4 %copy-start.1 = (f32[2,256,256]{2,1,0:T(8,128)}, f32[2,256,256]{2,1,0:T(8,128)S(1)}, u32[]{:S(2)}) copy-start(f32[2,256,256]{2,1,0:T(8,128)S(1)} %collective-permute-done.2.refs_1_.rest_3_.refs_2_) | copy-start | bytes 1572868
  21.3 30.5 %copy-start.2 = (f32[2,256,256]{2,1,0:T(8,128)}, f32[2,256,256]{2,1,0:T(8,128)S(1)}, u32[]{:S(2)}) copy-start(f32[2,256,256]{2,1,0:T(8,128)S(1)} %collective-permute-done.1.refs_2_.rest_2_.refs_3_) | copy-start | bytes 1572868
  21.3 24.1 %copy-start.3 = (f32[4,256,256]{2,1,0:T(8,128)}, f32[4,256,256]{2,1,0:T(8,128)S(1)}, u32[]{:S(2)}) copy-start(f32[4,256,256]{2,1,0:T(8,128)S(1)} %collective-permute-done.refs_5_.rest_1_) | copy-start | bytes 3145732
  21.8 27.4 %collective-permute-start.5 = (f32[8,256,256]{2,1,0:T(8,128)S(1)}, f32[8,256,256]{2,1,0:T(8,128)S(1)}, u32[]{:S(2)}, u32[]{:S(2)}) collective-permute-start(f32[8,256,256]{2,1,0:T(8,128)S(1)} %get-tuple-element.17), channel_id=1, source_target_pairs={{8,16},{24,32},{40,48},{16,8},{32,24},{48,40},{9,17},{25,33},{41,4... | collective-permute-start | bytes 6291464 | tf_op jit(solution)/shard_map/ppermute | solution.py:409
  24.3 21.1 %collective-permute-start.6 = (f32[3,256,256]{2,1,0:T(8,128)S(1)}, f32[3,256,256]{2,1,0:T(8,128)S(1)}, u32[]{:S(2)}, u32[]{:S(2)}) collective-permute-start(f32[3,256,256]{2,1,0:T(8,128)S(1)} %get-tuple-element.18), channel_id=1, source_target_pairs={{0,1},{1,2},{2,3},{3,4},{4,5},{5,6},{6,7},{8,9},{9,10},{10,11},{11... | collective-permute-start | bytes 2359304 | tf_op jit(solution)/shard_map/ppermute | solution.py:399
  27.9 19.6 %collective-permute-start.7 = (f32[3,256,256]{2,1,0:T(8,128)S(1)}, f32[3,256,256]{2,1,0:T(8,128)S(1)}, u32[]{:S(2)}, u32[]{:S(2)}) collective-permute-start(f32[3,256,256]{2,1,0:T(8,128)S(1)} %get-tuple-element.19), channel_id=1, source_target_pairs={{1,0},{2,1},{3,2},{4,3},{5,4},{6,5},{7,6},{9,8},{10,9},{11,10},{12... | collective-permute-start | bytes 2359304 | tf_op jit(solution)/shard_map/ppermute | solution.py:403
  29.2 14.8 %collective-permute-start.4 = (f32[2,256,256]{2,1,0:T(8,128)S(1)}, f32[2,256,256]{2,1,0:T(8,128)S(1)}, u32[]{:S(2)}, u32[]{:S(2)}) collective-permute-start(f32[2,256,256]{2,1,0:T(8,128)S(1)} %get-tuple-element.16), channel_id=1, source_target_pairs={{64,0},{128,64},{192,128},{65,1},{129,65},{193,129},{66,2},{130,66... | collective-permute-start | bytes 1572872 | tf_op jit(solution)/shard_map/ppermute | solution.py:403
  30.5 14.9 %collective-permute-start.3 = (f32[2,256,256]{2,1,0:T(8,128)S(1)}, f32[2,256,256]{2,1,0:T(8,128)S(1)}, u32[]{:S(2)}, u32[]{:S(2)}) collective-permute-start(f32[2,256,256]{2,1,0:T(8,128)S(1)} %get-tuple-element.16), channel_id=1, source_target_pairs={{0,64},{64,128},{128,192},{1,65},{65,129},{129,193},{2,66},{66,130... | collective-permute-start | bytes 1572872 | tf_op jit(solution)/shard_map/ppermute | solution.py:399
  44.0 7.9 %copy-start.6 = (f32[2,256,256]{2,1,0:T(8,128)}, f32[2,256,256]{2,1,0:T(8,128)S(1)}, u32[]{:S(2)}) copy-start(f32[2,256,256]{2,1,0:T(8,128)S(1)} %collective-permute-done.4.rest_5_.refs_4_) | copy-start | bytes 1572868
  45.4 6.4 %copy-start.7 = (f32[2,256,256]{2,1,0:T(8,128)}, f32[2,256,256]{2,1,0:T(8,128)S(1)}, u32[]{:S(2)}) copy-start(f32[2,256,256]{2,1,0:T(8,128)S(1)} %collective-permute-done.3.rest_4_.refs_5_) | copy-start | bytes 1572868
  45.4 6.4 %copy-start.4 = (f32[3,256,256]{2,1,0:T(8,128)}, f32[3,256,256]{2,1,0:T(8,128)S(1)}, u32[]{:S(2)}) copy-start(f32[3,256,256]{2,1,0:T(8,128)S(1)} %collective-permute-done.6.rest_7_.refs_1_) | copy-start | bytes 2359300
  47.5 4.4 %copy-start.5 = (f32[3,256,256]{2,1,0:T(8,128)}, f32[3,256,256]{2,1,0:T(8,128)S(1)}, u32[]{:S(2)}) copy-start(f32[3,256,256]{2,1,0:T(8,128)S(1)} %collective-permute-done.7.rest_8_.refs_0_) | copy-start | bytes 2359300
  49.1 3.3 %copy-start = (f32[8,256,256]{2,1,0:T(8,128)}, f32[8,256,256]{2,1,0:T(8,128)S(1)}, u32[]{:S(2)}) copy-start(f32[8,256,256]{2,1,0:T(8,128)S(1)} %collective-permute-done.5.rest_6_.refs_6_) | copy-start | bytes 6291460
  52.4 21.9 %collective-permute-start.11 = (f32[14,256,256]{2,1,0:T(8,128)}, f32[14,256,256]{2,1,0:T(8,128)}, u32[]{:S(2)}, u32[]{:S(2)}) collective-permute-start(f32[14,256,256]{2,1,0:T(8,128)} %get-tuple-element.25), channel_id=1, source_target_pairs={{0,8},{8,0},{16,24},{24,16},{32,40},{40,32},{48,56},{56,48},{1,9},... | collective-permute-start | bytes 11010056 | tf_op jit(solution)/shard_map/ppermute | solution.py:383
  52.4 21.9 %collective-permute-start.8 = (f32[6,256,256]{2,1,0:T(8,128)}, f32[6,256,256]{2,1,0:T(8,128)S(1)}, u32[]{:S(2)}, u32[]{:S(2)}) collective-permute-start(f32[6,256,256]{2,1,0:T(8,128)} %get-tuple-element.22), channel_id=1, source_target_pairs={{8,16},{24,32},{40,48},{16,8},{32,24},{48,40},{9,17},{25,33},{41,4... | collective-permute-start | bytes 4718600 | tf_op jit(solution)/shard_map/ppermute | solution.py:409
  55.7 17.6 %collective-permute-start.9 = (f32[2,256,256]{2,1,0:T(8,128)}, f32[2,256,256]{2,1,0:T(8,128)S(1)}, u32[]{:S(2)}, u32[]{:S(2)}) collective-permute-start(f32[2,256,256]{2,1,0:T(8,128)} %get-tuple-element.23), channel_id=1, source_target_pairs={{0,1},{1,2},{2,3},{3,4},{4,5},{5,6},{6,7},{8,9},{9,10},{10,11},{11... | collective-permute-start | bytes 1572872 | tf_op jit(solution)/shard_map/ppermute | solution.py:399
  59.3 14.1 %collective-permute-start.10 = (f32[2,256,256]{2,1,0:T(8,128)}, f32[2,256,256]{2,1,0:T(8,128)S(1)}, u32[]{:S(2)}, u32[]{:S(2)}) collective-permute-start(f32[2,256,256]{2,1,0:T(8,128)} %get-tuple-element.24), channel_id=1, source_target_pairs={{1,0},{2,1},{3,2},{4,3},{5,4},{6,5},{7,6},{9,8},{10,9},{11,10},{12... | collective-permute-start | bytes 1572872 | tf_op jit(solution)/shard_map/ppermute | solution.py:403
  74.3 1.2 copy-start.10
  75.5 0.7 copy-start.8
